TPU v7x, 256 devices: a whole 4x4x8 slice. The times are simulated.
256 devices in a mesh: dp: 16 (over y, z_lo, core), cuts: 16 (over x, z_hi).
Axes of the slice: x: 4, y: 4, z: 8 (z_hi: 4, z_lo: 2; z = z_hi * 2 + z_lo), core: 2. Of those that a mesh axis runs over, the one named last changes fastest.
Arguments:
- features: bfloat16 [16, 16, 1024, 768], P('dp', None, None, 'cuts'), may hold values from -6 to 6
- lists_one: int32 [16, 16, 192, 5], P('dp'), may hold values from 0 to 1023
- lists_two: int32 [16, 16, 160, 5], P('dp', 'cuts'), may hold values from 0 to 191
- lists_three: int32 [16, 16, 128, 3], P('dp', 'cuts'), may hold values from 0 to 159
- labels: int32 [16, 16, 128], P('dp', 'cuts'), may hold values from 0 to 152
- initial_node_weight: bfloat16 [768, 1024], P('cuts'), may hold values from -0.21875 to 0.21875
- initial_neighbour_weight: bfloat16 [768, 1024], P('cuts'), may hold values from -0.21875 to 0.21875
- second_self: bfloat16 [1024, 1024], replicated, may hold values from -0.1875 to 0.1875
- second_neigh: bfloat16 [1024, 1024], replicated, may hold values from -0.1875 to 0.1875
- final_node_weight: bfloat16 [1024, 153], replicated, may hold values from -0.1875 to 0.1875
- third_neigh: bfloat16 [1024, 153], replicated, may hold values from -0.1875 to 0.1875
Outputs:
- losses: float32 [16, 16], P('dp', 'cuts')
- grad_first_self: float32 [768, 1024], P('cuts')
- grad_first_neigh: float32 [768, 1024], P('cuts')
- grad_second_self: float32 [1024, 1024], P('cuts')
- grad_second_neigh: float32 [1024, 1024], P('cuts')
- grad_third_self: float32 [1024, 153], P('cuts')
- grad_third_neigh: float32 [1024, 153], P('cuts')
All inputs are finite; a program needn't handle non-finite values.
Results may differ from a plain program's by a relative error of at most 0.024.
Values may be sent and summed in bfloat16 or wider, within the bound.
A program may use at most 128 MiB of HBM per device.

v0:
```python
import jax
import jax.numpy as jnp
from jax import lax
from jax.sharding import PartitionSpec as P

FAN1 = 5
FAN2 = 5
FAN3 = 3
R1 = 192


def counting(indices, columns):
    hits = indices[:, :, None] == jnp.arange(columns, dtype=jnp.int32)[None, None, :]
    return jnp.sum(hits.astype(jnp.float32), axis=1).astype(jnp.bfloat16)


def aggregate(counts, source, fanout):
    summed = jnp.dot(counts, source, preferred_element_type=jnp.float32)
    return (summed * (1.0 / fanout)).astype(jnp.bfloat16)


def activate(values):
    return values * jax.nn.sigmoid(values)


def slope(values):
    sigma = jax.nn.sigmoid(values)
    return sigma * (1.0 + values * (1.0 - sigma))


def upper_layers(
    pre_one,
    lists_two,
    lists_three,
    seed_labels,
    second_self,
    second_neigh,
    final_node_weight,
    third_neigh,
):
    rows_one = pre_one.shape[0]
    rows_two = lists_two.shape[0]
    seed_count = lists_three.shape[0]
    act_one = activate(pre_one).astype(jnp.bfloat16)
    counts_two = counting(lists_two, rows_one)
    mean_two = aggregate(counts_two, act_one, FAN2)
    pre_two = jnp.dot(
        act_one[:rows_two], second_self, preferred_element_type=jnp.float32
    ) + jnp.dot(mean_two, second_neigh, preferred_element_type=jnp.float32)
    act_two = activate(pre_two).astype(jnp.bfloat16)
    counts_three = counting(lists_three, rows_two)
    mean_three = aggregate(counts_three, act_two, FAN3)
    logits = jnp.dot(
        act_two[:seed_count], final_node_weight, preferred_element_type=jnp.float32
    ) + jnp.dot(mean_three, third_neigh, preferred_element_type=jnp.float32)
    expon = jnp.exp(logits)
    combined_sums = jnp.sum(expon, axis=1, keepdims=True)
    onehot_labels = (
        seed_labels[:, None] == jnp.arange(logits.shape[1], dtype=jnp.int32)[None, :]
    ).astype(jnp.float32)
    mean_loss = jnp.mean(jnp.log(combined_sums[:, 0]) - jnp.sum(logits * onehot_labels, axis=1))
    grad_logits = ((expon / combined_sums - onehot_labels) * (1.0 / seed_count)).astype(
        jnp.bfloat16
    )
    grad_third_self = jnp.dot(
        act_two[:seed_count].T, grad_logits, preferred_element_type=jnp.float32
    )
    grad_third_neigh = jnp.dot(mean_three.T, grad_logits, preferred_element_type=jnp.float32)
    back_three = (
        jnp.dot(grad_logits, third_neigh.T, preferred_element_type=jnp.float32) * (1.0 / FAN3)
    ).astype(jnp.bfloat16)
    own_three = jnp.dot(grad_logits, final_node_weight.T, preferred_element_type=jnp.float32)
    grad_act_two = jnp.pad(own_three, ((0, rows_two - seed_count), (0, 0))) + jnp.dot(
        counts_three.T, back_three, preferred_element_type=jnp.float32
    )
    grad_pre_two = (grad_act_two * slope(pre_two)).astype(jnp.bfloat16)
    grad_second_self = jnp.dot(
        act_one[:rows_two].T, grad_pre_two, preferred_element_type=jnp.float32
    )
    grad_second_neigh = jnp.dot(mean_two.T, grad_pre_two, preferred_element_type=jnp.float32)
    back_two = (
        jnp.dot(grad_pre_two, second_neigh.T, preferred_element_type=jnp.float32) * (1.0 / FAN2)
    ).astype(jnp.bfloat16)
    own_two = jnp.dot(grad_pre_two, second_self.T, preferred_element_type=jnp.float32)
    grad_act_one = jnp.pad(own_two, ((0, rows_one - rows_two), (0, 0))) + jnp.dot(
        counts_two.T, back_two, preferred_element_type=jnp.float32
    )
    grad_pre_one = (grad_act_one * slope(pre_one)).astype(jnp.bfloat16)
    return (
        mean_loss,
        (grad_second_self, grad_second_neigh, grad_third_self, grad_third_neigh),
        grad_pre_one,
    )


def per_device(
    features,
    lists_one,
    lists_two,
    lists_three,
    labels,
    initial_node_weight,
    initial_neighbour_weight,
    second_self,
    second_neigh,
    final_node_weight,
    third_neigh,
):
    frontier = features[0]
    first_lists = lists_one[0]

    def one_mean(pair):
        return aggregate(counting(pair[0], pair[1].shape[0]), pair[1], FAN1)

    means_one = lax.map(one_mean, (first_lists, frontier))
    self_rows = frontier[:, :R1, :]
    node_own_term = self_rows
    neighbour_mean_term = means_one
    pre_one = lax.psum_scatter(
        jnp.einsum(
            "cnk,ke->cne", node_own_term, initial_node_weight, preferred_element_type=jnp.float32
        )
        + jnp.einsum(
            "cnk,ke->cne",
            neighbour_mean_term,
            initial_neighbour_weight,
            preferred_element_type=jnp.float32,
        ),
        "cuts",
        scatter_dimension=0,
        tiled=True,
    )[0]
    mean_loss, upper_grads, grad_pre_one = upper_layers(
        pre_one,
        lists_two[0, 0],
        lists_three[0, 0],
        labels[0, 0],
        second_self,
        second_neigh,
        final_node_weight,
        third_neigh,
    )
    feature_column_slice = lax.all_gather(grad_pre_one[None], "cuts", axis=0, tiled=True)
    node_own_term = self_rows
    neighbour_mean_term = means_one
    group_self = jnp.einsum(
        "pov,pox->vx", node_own_term, feature_column_slice, preferred_element_type=jnp.float32
    )
    group_neigh = jnp.einsum(
        "pov,pox->vx", neighbour_mean_term, feature_column_slice, preferred_element_type=jnp.float32
    )
    grad_first_self, grad_first_neigh = (
        lax.psum(group_self.astype(jnp.bfloat16), "dp").astype(jnp.float32),
        lax.psum(group_neigh.astype(jnp.bfloat16), "dp").astype(jnp.float32),
    )
    grad_second_self, grad_second_neigh, grad_third_self, grad_third_neigh = upper_grads
    sliced = (
        lax.psum_scatter(
            grad_second_self.astype(jnp.bfloat16), "cuts", scatter_dimension=0, tiled=True
        ).astype(jnp.float32),
        lax.psum_scatter(
            grad_second_neigh.astype(jnp.bfloat16), "cuts", scatter_dimension=0, tiled=True
        ).astype(jnp.float32),
        lax.psum_scatter(
            grad_third_self.astype(jnp.bfloat16), "cuts", scatter_dimension=0, tiled=True
        ).astype(jnp.float32),
        lax.psum_scatter(
            grad_third_neigh.astype(jnp.bfloat16), "cuts", scatter_dimension=0, tiled=True
        ).astype(jnp.float32),
    )
    summed = (
        lax.psum(sliced[0].astype(jnp.bfloat16), "dp").astype(jnp.float32),
        lax.psum(sliced[1].astype(jnp.bfloat16), "dp").astype(jnp.float32),
        lax.psum(sliced[2].astype(jnp.bfloat16), "dp").astype(jnp.float32),
        lax.psum(sliced[3].astype(jnp.bfloat16), "dp").astype(jnp.float32),
    )
    return (
        mean_loss.reshape(1, 1),
        grad_first_self,
        grad_first_neigh,
        summed[0],
        summed[1],
        summed[2],
        summed[3],
    )


def solution(mesh):
    return jax.shard_map(
        per_device,
        mesh=mesh,
        in_specs=(
            P("dp", None, None, "cuts"),
            P("dp", None, None, None),
            P("dp", "cuts", None, None),
            P("dp", "cuts", None, None),
            P("dp", "cuts", None),
            P("cuts", None),
            P("cuts", None),
            P(),
            P(),
            P(),
            P(),
        ),
        out_specs=(
            P("dp", "cuts"),
            P("cuts", None),
            P("cuts", None),
            P("cuts", None),
            P("cuts", None),
            P("cuts", None),
            P("cuts", None),
        ),
        check_vma=False,
    )
```

profile of v0, /device:TPU:1, one launch (start us, length us, event | category | flops | bytes accessed | tf_op | source)
XLA Modules:
  0.0 809.2 jit_solution(14408248699904036786)
XLA Ops:
  7.2 1.1 copy.34
  8.3 26.6 %while.10 = (s32[]{:T(128)}, bf16[16,192,48]{1,2,0:T(8,128)(2,1)S(1)}, s32[16,192,5]{1,2,0:T(8,128)S(1)}, bf16[16,1024,48]{1,2,0:T(8,128)(2,1)}, s32[]{:T(128)}) while((s32[]{:T(128)}, bf16[16,192,48]{1,2,0:T(8,128)(2,1)S(1)}, s32[16,192,5]{1,2,0:T(8,128)S(1)}, bf16[16,1024,48]{1,2,0:T(8,128)(2,1)}, s32[]{:T(128)}) %tuple.47), condition=%wide.region_2.3_spmd, body=%wide.region_0.2_spmd.sunk | while | flops 21645312 | bytes 921921 | solution.py:115
  8.8 1.1 fusion.81
  10.5 1.1 fusion.81
  12.2 1.1 fusion.81
  13.8 1.1 fusion.81
  15.5 1.1 fusion.81
  17.2 1.1 fusion.81
  18.8 1.1 fusion.81
  20.5 1.1 fusion.81
  22.2 1.1 fusion.81
  23.8 1.1 fusion.81
  25.5 1.1 fusion.81
  27.1 1.1 fusion.81
  28.8 1.1 fusion.81
  30.5 1.1 fusion.81
  32.1 1.1 fusion.81
  33.8 1.1 fusion.81
  35.0 2.9 fusion.25
  37.8 6.4 convolution_add_fusion
  45.1 163.6 %reduce-scatter.6.cloned.1.call-done = f32[1,192,1024]{2,1,0:T(8,128)} async-done(((f32[16,192,1024]{2,1,0:T(8,128)}), f32[1,192,1024]{2,1,0:T(8,128)}) %reduce-scatter.6.cloned.1.call-update) | async-done | bytes 786448 | tf_op jit(solution)/shard_map/reduce_scatter | solution.py:119
  208.8 1.3 fusion.21
  210.4 2.2 fusion.29
  212.7 1.4 multiply_convert_fusion
  214.6 0.8 exponential_reduce_fusion
  215.4 1.0 fusion.43
  216.5 1.9 fusion.11
  218.4 3.3 fusion.44
  221.7 3.3 fusion.9
  225.0 3.1 convolution_convert_fusion
  228.1 2.1 convolution_convert_fusion.1
  230.3 1.1 convolution_convert_fusion.2
  231.5 1.1 convolution_convert_fusion.3
  232.9 81.4 %all-gather.3.cloned.1.call-done = bf16[3072,1024]{1,0:T(8,128)(2,1)} async-done(((bf16[192,1024]{1,0:T(8,128)(2,1)}), bf16[3072,1024]{1,0:T(8,128)(2,1)}) %all-gather.3.cloned.1.call-update) | async-done | bytes 6291472 | tf_op jit(solution)/shard_map/all_gather | solution.py:143
  314.3 4.8 fusion.15
  319.1 2.9 fusion.17
  322.0 87.2 %reduce-scatter.10.cloned.1.call-done = bf16[64,1024]{1,0:T(8,128)(2,1)} async-done(((bf16[1024,1024]{1,0:T(8,128)(2,1)}), bf16[64,1024]{1,0:T(8,128)(2,1)}) %reduce-scatter.10.cloned.1.call-update) | async-done | bytes 131088 | tf_op jit(solution)/shard_map/reduce_scatter | solution.py:161
  409.2 89.8 %reduce-scatter.8.cloned.1.call-done = bf16[64,1024]{1,0:T(8,128)(2,1)} async-done(((bf16[1024,1024]{1,0:T(8,128)(2,1)}), bf16[64,1024]{1,0:T(8,128)(2,1)}) %reduce-scatter.8.cloned.1.call-update) | async-done | bytes 131088 | tf_op jit(solution)/shard_map/reduce_scatter | solution.py:158
  500.3 84.8 %reduce-scatter.14.cloned.1.call-done = bf16[64,153]{1,0:T(8,128)(2,1)} async-done(((bf16[1024,153]{1,0:T(8,128)(2,1)}), bf16[64,153]{1,0:T(8,128)(2,1)}) %reduce-scatter.14.cloned.1.call-update) | async-done | bytes 19600 | tf_op jit(solution)/shard_map/reduce_scatter | solution.py:167
  585.1 87.0 %reduce-scatter.12.cloned.1.call-done = bf16[64,153]{1,0:T(8,128)(2,1)} async-done(((bf16[1024,153]{1,0:T(8,128)(2,1)}), bf16[64,153]{1,0:T(8,128)(2,1)}) %reduce-scatter.12.cloned.1.call-update) | async-done | bytes 19600 | tf_op jit(solution)/shard_map/reduce_scatter | solution.py:164
  672.2 52.1 %all-reduce.2 = (bf16[64,153]{1,0:T(8,128)(2,1)S(1)}, bf16[64,153]{1,0:T(8,128)(2,1)S(1)}) all-reduce(bf16[64,153]{1,0:T(8,128)(2,1)} %reduce-scatter.12.cloned.1.call-done, bf16[64,153]{1,0:T(8,128)(2,1)} %reduce-scatter.14.cloned.1.call-done), channel_id=1, replica_groups=mesh['dp'=16,'cuts'=16] {'dp'}, use_global_device_ids=true, to_apply=%region_16.17 | all-reduce | flops 19584 | bytes 78336 | tf_op jit(solution)/shard_map/psum | solution.py:174
  724.2 0.6 convert_element_type.126
  724.9 0.6 convert_element_type.128
  725.5 69.3 %all-reduce.6.cloned.1.call-done = (bf16[48,1024]{1,0:T(8,128)(2,1)}, bf16[48,1024]{1,0:T(8,128)(2,1)}, bf16[64,1024]{1,0:T(8,128)(2,1)}, bf16[64,1024]{1,0:T(8,128)(2,1)}) async-done(((bf16[48,1024]{1,0:T(8,128)(2,1)}, bf16[48,1024]{1,0:T(8,128)(2,1)}, bf16[64,1024]{1,0:T(8,128)(2,1)}, bf16[64,1024]{1,0:T(8,128)(2,1)}), (bf16[48,1024]{1,0:T(8,128)(2,1)}, bf16[48,1024]{1,0:T(8,128)(2,1)}, ...) | async-done | bytes 458768 | tf_op jit(solution)/shard_map/psum | solution.py:153
  794.8 1.6 convert_element_type.122
  796.4 1.6 convert_element_type.124
  798.0 1.6 convert_element_type.118
  799.6 1.6 convert_element_type.120
  (88 shorter events, 10.7 us)
Async XLA Ops:
  7.2 205.5 %copy-start = (bf16[1024,1024]{1,0:T(8,128)(2,1)S(1)}, bf16[1024,1024]{1,0:T(8,128)(2,1)}, u32[]{:S(2)}) copy-start(bf16[1024,1024]{1,0:T(8,128)(2,1)} %param.21) | copy-start | bytes 6291460
  7.2 201.6 %reduce-scatter.6.cloned.1.call-start = ((), (), s32[]{:S(2)}) async-start(), calls=%async_computation.5 | async-start | bytes 13369344 | tf_op jit(solution)/shard_map/reduce_scatter | solution.py:119
  8.3 26.6 %copy-start.8 = (bf16[48,1024]{1,0:T(8,128)(2,1)S(1)}, bf16[48,1024]{1,0:T(8,128)(2,1)}, u32[]{:S(2)}) copy-start(bf16[48,1024]{1,0:T(8,128)(2,1)} %param.18) | copy-start | bytes 294916
  35.0 2.9 copy-start.9
  44.2 0.7 copy-start.10
  44.2 0.7 copy-start.14
  44.2 270.0 %all-gather.3.cloned.1.call-start = ((), (), s32[]{:S(2)}) async-start(), calls=%async_computation.10 | async-start | bytes 6684672 | tf_op jit(solution)/shard_map/all_gather | solution.py:143
  45.1 167.5 %copy-start.7 = (bf16[160,192]{1,0:T(8,128)(2,1)}, bf16[160,192]{1,0:T(8,128)(2,1)S(1)}, u32[]{:S(2)}) copy-start(bf16[160,192]{1,0:T(8,128)(2,1)S(1)} %convert_reduce_fusion.1) | copy-start | bytes 184324
  210.4 3.7 copy-start.5
  212.7 1.7 copy-start.4
  212.7 1.9 copy-start.6
  212.7 1.9 copy-start.11
  214.1 2.4 copy-start.2
  215.4 1.1 copy-start.12
  224.9 184.2 %reduce-scatter.10.cloned.1.call-start = ((), (), s32[]{:S(2)}) async-start(), calls=%async_computation.7 | async-start | bytes 2228224 | tf_op jit(solution)/shard_map/reduce_scatter | solution.py:161
  228.1 270.9 %reduce-scatter.8.cloned.1.call-start = ((), (), s32[]{:S(2)}) async-start(), calls=%async_computation.6 | async-start | bytes 2228224 | tf_op jit(solution)/shard_map/reduce_scatter | solution.py:158
  230.2 1.3 copy-start.3
  230.3 354.9 %reduce-scatter.14.cloned.1.call-start = ((), (), s32[]{:S(2)}) async-start(), calls=%async_computation.9 | async-start | bytes 557056 | tf_op jit(solution)/shard_map/reduce_scatter | solution.py:167
  231.5 440.7 %reduce-scatter.12.cloned.1.call-start = ((), (), s32[]{:S(2)}) async-start(), calls=%async_computation.8 | async-start | bytes 557056 | tf_op jit(solution)/shard_map/reduce_scatter | solution.py:164
  232.7 562.1 %all-reduce.6.cloned.1.call-start = ((), (), s32[]{:S(2)}) async-start(), calls=%async_computation.11 | async-start | bytes 917504 | tf_op jit(solution)/shard_map/psum | solution.py:153
  314.3 4.8 copy-start.1
  319.1 179.9 %copy-start.13 = (f32[128]{0:T(128)S(1)}, f32[128]{0:T(128)}, u32[]{:S(2)}) copy-start(f32[128]{0:T(128)} %copy-done.12) | copy-start | bytes 1540
  319.1 179.9 %copy-start.15 = (f32[128]{0:T(128)S(1)}, f32[128]{0:T(128)}, u32[]{:S(2)}) copy-start(f32[128]{0:T(128)} %get-tuple-element.43) | copy-start | bytes 1540
Sparse Core Ops, SparseCore 0:
  44.4 164.3 reduce-scatter.5
  225.1 89.1 all-gather.2
  317.8 91.3 reduce-scatter.9
  413.0 85.9 reduce-scatter.7
  502.3 82.7 reduce-scatter.13
  588.9 83.2 reduce-scatter.11
  675.6 119.1 all-reduce.5
where the time goes:
time: 810 us; the launch traced here: 809 us
  waiting for transfers between devices  663 us (82%)
  matrix products  57.2 us (7%)
  blocking collectives  52.1 us (6%)
  other arithmetic  17.6 us (2%)
  between operations  16.1 us (2%)
    reduce_scatter x1, waiting for transfers between devices, per_device(): lax.psum_scatter(jnp.einsum('cnk,ke->cne', node_own_term, initial_node_we...  164 us
    reduce_scatter x1, waiting for transfers between devices, per_device(): lax.psum_scatter(grad_second_self.astype(jnp.bfloat16), 'cuts', scatter_d...  89.8 us
    reduce_scatter x1, waiting for transfers between devices, per_device(): lax.psum_scatter(grad_second_neigh.astype(jnp.bfloat16), 'cuts', scatter_...  87.2 us
    reduce_scatter x1, waiting for transfers between devices, per_device(): lax.psum_scatter(grad_third_self.astype(jnp.bfloat16), 'cuts', scatter_di...  87 us
    reduce_scatter x1, waiting for transfers between devices, per_device(): lax.psum_scatter(grad_third_neigh.astype(jnp.bfloat16), 'cuts', scatter_d...  84.8 us
    all_gather x1, waiting for transfers between devices, per_device(): lax.all_gather(grad_pre_one[None], 'cuts', axis=0, tiled=True)  81.4 us
    psum x1, waiting for transfers between devices, per_device(): lax.psum(group_self.astype(jnp.bfloat16), 'dp').astype(jnp.float32)  69.3 us
    psum x1, blocking collectives, per_device(): lax.psum(sliced[2].astype(jnp.bfloat16), 'dp').astype(jnp.float32)  52.1 us
  transfers between devices with their start and end apart: 7, of which 7 were waited for; matrix products, arithmetic and copies ran while one was open for 2% of the time, Pallas kernels for 0%

commit v1 on v0

v1 whole, which is shorter than its diff:
```python
import jax
import jax.numpy as jnp
from jax import lax
from jax.experimental import pallas as pl
from jax.experimental.pallas import tpu as pltpu
from jax.sharding import PartitionSpec as P

MESH = pl.DeviceIdType.MESH
BF = jnp.bfloat16
F32 = jnp.float32
FAN1 = 5
FAN2 = 5
FAN3 = 3
R0 = 1024
R1 = 192
R2 = 160
SEEDS = 128
HID = 1024
CUTS = 16
WIDE = 48
CLASSES = 153
PADDED = 256
VMEM = pl.BlockSpec(memory_space=pltpu.VMEM)


def place():
    d, c = lax.axis_index("dp"), lax.axis_index("cuts")
    return c // 4, d // 4, c % 4, (d // 2) % 2, d % 2


def device(x, y, zh, zl, k):
    return {"dp": (y * 2 + zl) * 2 + k, "cuts": x * 4 + zh}


def remote(src, dst, send, recv, to):
    return pltpu.make_async_remote_copy(
        src_ref=src, dst_ref=dst, send_sem=send, recv_sem=recv, device_id=to, device_id_type=MESH
    )


def gather_kernel(
    lists, xt, w_self, w_neigh, at, w,
    blk_out, blk_in, half,
    a_send, a_recv, wz_send, wz_recv, wx_send, wx_recv, wk_send, wk_recv,
):
    x, y, zh, zl, k = place()
    me = x * 4 + zh
    sibling = device(x, y, zh, zl, 1 - k)

    barrier = pltpu.get_barrier_semaphore()
    for s in range(1, CUTS):
        pl.semaphore_signal(
            barrier, 1, device_id={"dp": lax.axis_index("dp"), "cuts": (me + s) % CUTS},
            device_id_type=MESH,
        )
    pl.semaphore_signal(barrier, 1, device_id=sibling, device_id_type=MESH)
    pl.semaphore_wait(barrier, CUTS)

    half[...] = jnp.where(k == 0, w_self[...], w_neigh[...])
    w[0, me] = w_self[...]
    w[1, me] = w_neigh[...]
    sends = []
    for s in range(1, 4):
        cp = remote(
            half, w.at[k, me], wz_send.at[s - 1], wz_recv.at[s - 1],
            device(x, y, (zh + s) % 4, zl, k),
        )
        cp.start()
        sends.append(cp)

    def spread_x(j):
        src = x * 4 + (zh + 4 - j) % 4
        for s in range(1, 4):
            n = j * 3 + s - 1
            cp = remote(
                w.at[k, src] if j else half, w.at[k, src], wx_send.at[n], wx_recv.at[n],
                device((x + s) % 4, y, zh, zl, k),
            )
            cp.start()
            sends.append(cp)

    def spread_core(n, src):
        cp = remote(w.at[k, src], w.at[k, src], wk_send.at[n], wk_recv.at[n], sibling)
        cp.start()
        sends.append(cp)

    spread_x(0)

    def block(m):
        idx = lists[:, pl.ds(m, 1), :]
        rows = lax.broadcasted_iota(jnp.int32, (R0, R1), 0)
        counts = jnp.zeros((R0, R1), F32)
        for f in range(FAN1):
            counts = counts + jnp.where(rows == idx[f], 1.0, 0.0)
        mean = jnp.dot(xt[m], counts.astype(BF), preferred_element_type=F32)
        mean = (mean * (1.0 / FAN1)).astype(BF)
        own = xt[m][:, :R1]
        return own, mean

    def pack(ref, m, own, mean):
        ref[m, 0:48] = own[:, 0:128]
        ref[m, 48:96] = mean[:, 0:128]
        ref[m, 96:144] = jnp.concatenate([own[:, 128:192], mean[:, 128:192]], axis=1)

    def a_copy(s):
        m = (me + s) % CUTS
        return remote(
            blk_out.at[m], blk_in.at[me], a_send.at[s - 1], a_recv.at[s - 1],
            {"dp": lax.axis_index("dp"), "cuts": m},
        )

    def one(s, _):
        m = (me + s) % CUTS
        own, mean = block(m)
        pack(blk_out, m, own, mean)
        a_copy(s).start()
        return 0

    def z_arrival(j):
        remote(
            half, w.at[k, x * 4 + (zh + 4 - j) % 4], wz_send.at[j - 1], wz_recv.at[j - 1], sibling
        ).wait_recv()
        spread_x(j)
        spread_core(j - 1, x * 4 + (zh + 4 - j) % 4)

    lax.fori_loop(1, 6, one, 0)
    z_arrival(1)
    lax.fori_loop(6, 9, one, 0)
    z_arrival(3)
    lax.fori_loop(9, 12, one, 0)
    z_arrival(2)
    lax.fori_loop(12, 16, one, 0)
    own, mean = block(me)
    pack(blk_in, me, own, mean)

    for j in (0, 1, 3, 2):
        for s in range(1, 4):
            n = j * 3 + s - 1
            src = ((x + 4 - s) % 4) * 4 + (zh + 4 - j) % 4
            remote(half, w.at[k, src], wx_send.at[n], wx_recv.at[n], sibling).wait_recv()
            spread_core(3 + n, src)

    for s in range(1, CUTS):
        frm = (me + CUTS - s) % CUTS
        remote(blk_out.at[frm], blk_in.at[frm], a_send.at[s - 1], a_recv.at[s - 1], sibling).wait_recv()
    for c in range(CUTS):
        tail = blk_in[c, 96:144]
        at[0, c * 48:(c + 1) * 48, 0:128] = blk_in[c, 0:48]
        at[1, c * 48:(c + 1) * 48, 0:128] = blk_in[c, 48:96]
        at[0, c * 48:(c + 1) * 48, 128:192] = tail[:, 0:64]
        at[1, c * 48:(c + 1) * 48, 128:192] = tail[:, 64:128]

    for j in range(1, 4):
        remote(half, w.at[1 - k, x * 4 + (zh + 4 - j) % 4], wk_send.at[j - 1], wk_recv.at[j - 1], sibling).wait_recv()
    for j in range(4):
        for s in range(1, 4):
            n = j * 3 + s - 1
            src = ((x + 4 - s) % 4) * 4 + (zh + 4 - j) % 4
            remote(half, w.at[1 - k, src], wk_send.at[3 + n], wk_recv.at[3 + n], sibling).wait_recv()
    for cp in sends:
        cp.wait_send()

    def sent(s, _):
        a_copy(s).wait_send()
        return 0

    lax.fori_loop(1, CUTS, sent, 0)


def gather(lists, xt, w_self, w_neigh):
    dma = pltpu.SemaphoreType.DMA
    return pl.pallas_call(
        gather_kernel,
        out_shape=(
            jax.ShapeDtypeStruct((2, CUTS * WIDE, R1), BF),
            jax.ShapeDtypeStruct((2, CUTS, WIDE, HID), BF),
        ),
        in_specs=[VMEM] * 4,
        out_specs=(VMEM, VMEM),
        scratch_shapes=[
            pltpu.VMEM((CUTS, 144, 128), BF),
            pltpu.VMEM((CUTS, 144, 128), BF),
            pltpu.VMEM((WIDE, HID), BF),
            dma((15,)), dma((15,)), dma((3,)), dma((3,)), dma((12,)), dma((12,)), dma((15,)), dma((15,)),
        ],
        compiler_params=pltpu.CompilerParams(
            collective_id=1, has_side_effects=True, vmem_limit_bytes=48 * 2**20
        ),
    )(lists, xt, w_self, w_neigh)


def reduce_kernel(
    a1, a2, a3, g1, g2, g3, out,
    ra1, ra2, ra3, rg1, rg2, rg3,
    s_buf, r_one, r_x, t1, t2, r_two, u, r_z,
    c_send, c_recv, s1_send, s1_recv, s2_send, s2_recv, z_send, z_recv, f_send, f_recv, k_send, k_recv,
):
    x, y, zh, zl, k = place()
    sibling = device(x, y, zh, zl, 1 - k)
    xs = [(x + s) % 4 for s in range(4)]
    ys = [(y + s) % 4 for s in range(4)]
    zpos = zl * 4 + zh

    def z_peer(s):
        p = (zpos + s) % 8
        return p // 4, p % 4

    def f_peer(s):
        p = (y * 2 + zl + s) % 8
        return p // 2, p % 2

    barrier = pltpu.get_barrier_semaphore()
    peers = [sibling]
    peers += [device(xs[s], y, zh, zl, k) for s in range(1, 4)]
    for s in range(1, 8):
        pzl, pzh = z_peer(s)
        peers.append(device(x, y, pzh, pzl, k))
    for s in range(1, 8):
        py, pzl = f_peer(s)
        peers.append(device(x, py, zh, pzl, k))
    for p in peers:
        pl.semaphore_signal(barrier, 1, device_id=p, device_id_type=MESH)
    pl.semaphore_wait(barrier, len(peers))

    sends = []

    def go(cp):
        cp.start()
        sends.append(cp)

    pairs = ((a3.at[1 - k], ra3), (g3, rg3), (a2.at[1 - k], ra2), (g2, rg2), (a1.at[1 - k], ra1), (g1, rg1))
    swaps = []
    for i, (src, dst) in enumerate(pairs):
        cp = remote(src, dst, c_send.at[i], c_recv.at[i], sibling)
        go(cp)
        swaps.append(cp)

    def products(a_own, g_own, a_sib, g_sib, lanes):
        return (
            jnp.dot(a_own, g_own[:, lanes], preferred_element_type=F32)
            + jnp.dot(a_sib, g_sib[:, lanes], preferred_element_type=F32)
        ).astype(BF)

    swaps[0].wait_recv()
    swaps[1].wait_recv()
    third = products(a3[k].T, g3, ra3[...].T, rg3, slice(0, 256)).reshape(CUTS, 4, 16, 256)
    for j in range(4):
        s_buf[j // 2, 7, :, :, (j % 2) * 256:(j % 2 + 1) * 256] = third[:, j]
    swaps[2].wait_recv()
    swaps[3].wait_recv()
    a_own, a_sib = a2[k].T, ra2[...].T
    for n in range(4):
        p = products(a_own, g2, a_sib, rg2, slice(n * 256, (n + 1) * 256)).reshape(CUTS, 4, 16, 256)
        for g in range(4):
            s_buf[n // 2, 3 + g, :, :, (n % 2) * 256:(n % 2 + 1) * 256] = p[:, g]
    swaps[4].wait_recv()
    swaps[5].wait_recv()
    a_own, a_sib = a1[k], ra1[...]
    for n in range(4):
        p = products(a_own, g1, a_sib, rg1, slice(n * 256, (n + 1) * 256)).reshape(CUTS, 3, 16, 256)
        for g in range(3):
            s_buf[n // 2, g, :, :, (n % 2) * 256:(n % 2 + 1) * 256] = p[:, g]

    one = []
    for s in range(1, 4):
        cp = remote(
            s_buf.at[0, pl.ds(ys[s] * 2, 2)], r_one.at[s - 1], s1_send.at[s - 1], s1_recv.at[s - 1],
            device(x, ys[s], zh, zl, k),
        )
        go(cp)
        one.append(cp)
    for s in range(1, 4):
        cp = remote(
            s_buf.at[1, :, pl.ds(xs[s] * 4, 4)],
            r_x.at[s - 1],
            s1_send.at[s + 2], s1_recv.at[s + 2],
            device(xs[s], y, zh, zl, k),
        )
        go(cp)
        one.append(cp)
    for cp in one:
        cp.wait_recv()

    def add_y(c, _):
        for q in range(2):
            v = s_buf[0, y * 2 + q, c].astype(F32)
            for s in range(3):
                v = v + r_one[s, q, c].astype(F32)
            t1[q, c] = v.astype(BF)
        return 0

    lax.fori_loop(0, CUTS, add_y, 0)

    def add_x(g, _):
        for h in range(4):
            v = s_buf[1, g, x * 4 + h].astype(F32)
            for s in range(3):
                v = v + r_x[s, g, h].astype(F32)
            t2[g, h] = v.astype(BF)
        return 0

    lax.fori_loop(0, 8, add_x, 0)

    two = []
    for s in range(1, 4):
        cp = remote(
            t1.at[:, pl.ds(xs[s] * 4, 4)], r_two.at[0, s - 1], s2_send.at[s - 1], s2_recv.at[s - 1],
            device(xs[s], y, zh, zl, k),
        )
        go(cp)
        two.append(cp)
    for s in range(1, 4):
        cp = remote(
            t2.at[pl.ds(ys[s] * 2, 2)], r_two.at[1, s - 1], s2_send.at[s + 2], s2_recv.at[s + 2],
            device(x, ys[s], zh, zl, k),
        )
        go(cp)
        two.append(cp)
    for cp in two:
        cp.wait_recv()
    for q in range(2):
        for h in range(4):
            v = t1[q, x * 4 + h].astype(F32)
            for s in range(3):
                v = v + r_two[0, s, q, h].astype(F32)
            u[q, h, :, 0:512] = v.astype(BF)
            v = t2[y * 2 + q, h].astype(F32)
            for s in range(3):
                v = v + r_two[1, s, q, h].astype(F32)
            u[q, h, :, 512:1024] = v.astype(BF)

    zs = []
    for s in range(1, 8):
        pzl, pzh = z_peer(s)
        cp = remote(
            u.at[pzl, pzh], r_z.at[s - 1], z_send.at[s - 1], z_recv.at[s - 1], device(x, y, pzh, pzl, k)
        )
        go(cp)
        zs.append(cp)
    for cp in zs:
        cp.wait_recv()
    v = u[zl, zh].astype(F32)
    for s in range(7):
        v = v + r_z[s].astype(F32)
    mine = y * 2 + zl
    out[k, mine] = v.astype(BF)

    for s in range(1, 8):
        py, pzl = f_peer(s)
        go(remote(out.at[k, mine], out.at[k, mine], f_send.at[s - 1], f_recv.at[s - 1], device(x, py, zh, pzl, k)))
    for s in range(1, 8):
        frm = (mine + 8 - s) % 8
        remote(out.at[k, frm], out.at[k, frm], f_send.at[s - 1], f_recv.at[s - 1], sibling).wait_recv()
    last = remote(out.at[k], out.at[k], k_send.at[0], k_recv.at[0], sibling)
    go(last)
    remote(out.at[1 - k], out.at[1 - k], k_send.at[0], k_recv.at[0], sibling).wait_recv()
    for cp in sends:
        cp.wait_send()


def reduce_grads(a1, a2, a3, g1, g2, g3):
    dma = pltpu.SemaphoreType.DMA
    vm = lambda *shape: pltpu.VMEM(shape, BF)
    return pl.pallas_call(
        reduce_kernel,
        out_shape=jax.ShapeDtypeStruct((2, 8, 16, HID), BF),
        in_specs=[VMEM] * 6,
        out_specs=VMEM,
        scratch_shapes=[
            vm(CUTS * WIDE, R1), vm(R2, HID), vm(SEEDS, HID), vm(R1, HID), vm(R2, HID), vm(SEEDS, PADDED),
            vm(2, 8, CUTS, 16, 512),
            vm(3, 2, CUTS, 16, 512), vm(3, 8, 4, 16, 512),
            vm(2, CUTS, 16, 512),
            vm(8, 4, 16, 512),
            vm(2, 3, 2, 4, 16, 512),
            vm(2, 4, 16, HID),
            vm(7, 16, HID),
            dma((6,)), dma((6,)), dma((6,)), dma((6,)), dma((6,)), dma((6,)), dma((7,)), dma((7,)),
            dma((7,)), dma((7,)), dma((1,)), dma((1,)),
        ],
        compiler_params=pltpu.CompilerParams(
            collective_id=2, has_side_effects=True, vmem_limit_bytes=56 * 2**20
        ),
    )(a1, a2, a3, g1, g2, g3)


def finish_kernel(sums, first_self, first_neigh, second_self, second_neigh, third_self, third_neigh):
    for k, first, second, third in ((0, first_self, second_self, third_self), (1, first_neigh, second_neigh, third_neigh)):
        first[...] = sums[k, 0:3].reshape(48, HID).astype(F32)
        second[...] = sums[k, 3:7].reshape(64, HID).astype(F32)
        for j in range(4):
            third[j * 16:(j + 1) * 16] = sums[k, 7][:, j * 256:j * 256 + CLASSES].astype(F32)


def finish(sums):
    shapes = ((48, HID), (48, HID), (64, HID), (64, HID), (64, CLASSES), (64, CLASSES))
    return pl.pallas_call(
        finish_kernel,
        out_shape=tuple(jax.ShapeDtypeStruct(s, F32) for s in shapes),
        in_specs=[VMEM],
        out_specs=(VMEM,) * 6,
    )(sums)


def counting(indices, columns):
    hits = indices[:, :, None] == jnp.arange(columns, dtype=jnp.int32)[None, None, :]
    return jnp.sum(hits.astype(F32), axis=1).astype(BF)


def aggregate(counts, source, fanout):
    summed = jnp.dot(counts, source, preferred_element_type=F32)
    return (summed * (1.0 / fanout)).astype(BF)


def activate(values):
    return values * jax.nn.sigmoid(values)


def slope(values):
    sigma = jax.nn.sigmoid(values)
    return sigma * (1.0 + values * (1.0 - sigma))


def upper_layers(pre_one, lists_two, lists_three, seed_labels, second_self, second_neigh, final_node_weight, third_neigh):
    act_one = activate(pre_one).astype(BF)
    counts_two = counting(lists_two, R1)
    mean_two = aggregate(counts_two, act_one, FAN2)
    pre_two = jnp.dot(act_one[:R2], second_self, preferred_element_type=F32) + jnp.dot(
        mean_two, second_neigh, preferred_element_type=F32
    )
    act_two = activate(pre_two).astype(BF)
    counts_three = counting(lists_three, R2)
    mean_three = aggregate(counts_three, act_two, FAN3)
    logits = jnp.dot(act_two[:SEEDS], final_node_weight, preferred_element_type=F32) + jnp.dot(
        mean_three, third_neigh, preferred_element_type=F32
    )
    expon = jnp.exp(logits)
    sums = jnp.sum(expon, axis=1, keepdims=True)
    onehot = (seed_labels[:, None] == jnp.arange(CLASSES, dtype=jnp.int32)[None, :]).astype(F32)
    mean_loss = jnp.mean(jnp.log(sums[:, 0]) - jnp.sum(logits * onehot, axis=1))
    grad_logits = ((expon / sums - onehot) * (1.0 / SEEDS)).astype(BF)
    back_three = (jnp.dot(grad_logits, third_neigh.T, preferred_element_type=F32) * (1.0 / FAN3)).astype(BF)
    own_three = jnp.dot(grad_logits, final_node_weight.T, preferred_element_type=F32)
    grad_act_two = jnp.pad(own_three, ((0, R2 - SEEDS), (0, 0))) + jnp.dot(
        counts_three.T, back_three, preferred_element_type=F32
    )
    grad_pre_two = (grad_act_two * slope(pre_two)).astype(BF)
    back_two = (jnp.dot(grad_pre_two, second_neigh.T, preferred_element_type=F32) * (1.0 / FAN2)).astype(BF)
    own_two = jnp.dot(grad_pre_two, second_self.T, preferred_element_type=F32)
    grad_act_one = jnp.pad(own_two, ((0, R1 - R2), (0, 0))) + jnp.dot(
        counts_two.T, back_two, preferred_element_type=F32
    )
    grad_pre_one = (grad_act_one * slope(pre_one)).astype(BF)
    a2 = jnp.stack([act_one[:R2], mean_two])
    a3 = jnp.stack([act_two[:SEEDS], mean_three])
    g3 = jnp.pad(grad_logits, ((0, 0), (0, PADDED - CLASSES)))
    return mean_loss, a2, a3, grad_pre_one, grad_pre_two, g3


def per_device(
    features, lists_one, lists_two, lists_three, labels, initial_node_weight, initial_neighbour_weight,
    second_self, second_neigh, final_node_weight, third_neigh,
):
    xt = jnp.swapaxes(features[0], 1, 2)
    lists = jnp.transpose(lists_one[0], (2, 0, 1))
    at, w = gather(lists, xt, initial_node_weight, initial_neighbour_weight)
    pre_one = lax.dot_general(
        at.reshape(2 * CUTS * WIDE, R1), w.reshape(2 * CUTS * WIDE, HID), (((0,), (0,)), ((), ())),
        preferred_element_type=F32,
    )
    mean_loss, a2, a3, g1, g2, g3 = upper_layers(
        pre_one, lists_two[0, 0], lists_three[0, 0], labels[0, 0],
        second_self, second_neigh, final_node_weight, third_neigh,
    )
    sums = reduce_grads(at, a2, a3, g1, g2, g3)
    return (mean_loss.reshape(1, 1),) + tuple(finish(sums))


def solution(mesh):
    return jax.shard_map(
        per_device,
        mesh=mesh,
        in_specs=(
            P("dp", None, None, "cuts"),
            P("dp", None, None, None),
            P("dp", "cuts", None, None),
            P("dp", "cuts", None, None),
            P("dp", "cuts", None),
            P("cuts", None),
            P("cuts", None),
            P(), P(), P(), P(),
        ),
        out_specs=(P("dp", "cuts"),) + (P("cuts", None),) * 6,
        check_vma=False,
    )
```

time: 810 us -> 130 us (0.16)
  waiting for transfers between devices: 663 us -> 0 us
  Pallas kernels: 0 us -> 104 us
  blocking collectives: 52.1 us -> 0 us
  matrix products: 57.2 us -> 15.6 us
  other arithmetic: 17.6 us -> 2.7 us
  between operations: 16.1 us -> 2.62 us
    reduce_scatter x5 -> x0, waiting for transfers between devices: 513 us -> none  [the longest x1 164 us: per_device(): lax.psum_scatter(jnp.einsum('cnk,ke->cne', node_own_term, initial_node_we...]
    pallas_call x0 -> x3, Pallas kernels: none -> 104 us  [the longest x1 64 us: reduce_grads(): pl.pallas_call(reduce_kernel, out_shape=jax.ShapeDtypeStruct((2, 8, 16, H...]
    all_gather x1 -> x0, waiting for transfers between devices: 81.4 us -> none  [per_device(): lax.all_gather(grad_pre_one[None], 'cuts', axis=0, tiled=True)]
    psum x1 -> x0, waiting for transfers between devices: 69.3 us -> none  [per_device(): lax.psum(group_self.astype(jnp.bfloat16), 'dp').astype(jnp.float32)]
    psum x1 -> x0, blocking collectives: 52.1 us -> none  [per_device(): lax.psum(sliced[2].astype(jnp.bfloat16), 'dp').astype(jnp.float32)]
    dot_general x34 -> x11, matrix products: 57.2 us -> 15.6 us  [the longest x1 3.39 us: upper_layers(): own_two = jnp.dot(grad_pre_two, second_self.T, preferred_element_type=F32)]
    convert_element_type x8 -> x1, other arithmetic: 9.06 us -> 0.11 us  [upper_layers(): grad_logits = ((expon / sums - onehot) * (1.0 / SEEDS)).astype(BF)]
  transfers between devices with their start and end apart: 7 -> 0, of which waited for: 7 -> 0; matrix products, arithmetic and copies ran while one was open for 2% -> 0% of each run, Pallas kernels for 0% -> 0%
where the time goes in v1:
time: 130 us
  Pallas kernels  104 us (80%)
  matrix products  15.6 us (12%)
  local copies, waits for them, and re-layouts  4.97 us (4%)
  other arithmetic  2.7 us (2%)
  between operations  2.62 us (2%)
    pallas_call x1, Pallas kernels, reduce_grads(): pl.pallas_call(reduce_kernel, out_shape=jax.ShapeDtypeStruct((2, 8, 16, H...  64 us
    pallas_call x1, Pallas kernels, gather(): pl.pallas_call(gather_kernel, out_shape=(jax.ShapeDtypeStruct((2, CUTS *...  37.9 us
    unnamed x34, local copies, waits for them, and re-layouts  4.29 us
    dot_general x1, matrix products, upper_layers(): own_two = jnp.dot(grad_pre_two, second_self.T, preferred_element_type=F32)  3.39 us
    dot_general x1, matrix products, upper_layers(): jnp.dot(counts_two.T, back_two, preferred_element_type=F32)  3.34 us

profile of v1, /device:TPU:1, one launch (start us, length us, event | category | flops | bytes accessed | tf_op | source)
XLA Modules:
  0.0 129.8 jit_solution(17506055889285031401)
XLA Ops:
  0.6 0.0 copy-start
  0.6 0.0 copy-start.1
  0.7 1.5 %copy-done.1 = bf16[1,16,1024,48]{2,3,1,0:T(8,128)(2,1)S(1)} copy-done((bf16[1,16,1024,48]{2,3,1,0:T(8,128)(2,1)S(1)}, bf16[1,16,1024,48]{2,3,1,0:T(8,128)(2,1)}, u32[]{:S(2)}) %copy-start.1) | copy-done | bytes 1572888
  2.2 0.0 copy-start.3
  2.2 0.9 copy-done.3
  3.1 0.0 copy-start.4
  3.1 0.9 copy-done.4
  4.0 0.9 copy-done.5
  4.9 37.9 %shard_map.162 = (bf16[2,768,192]{2,1,0:T(8,128)(2,1)S(1)}, bf16[2,16,48,1024]{3,2,1,0:T(8,128)(2,1)S(1)}) custom-call(s32[5,16,192]{2,1,0:T(8,128)S(1)} %bitcast.46, bf16[16,48,1024]{2,1,0:T(8,128)(2,1)S(1)} %bitcast.44, bf16[48,1024]{1,0:T(8,128)(2,1)S(1)} %copy-done.3, bf16[48,1024]{1,0:T(8,128)(2,1)S(1)} %copy-done.4), custom_call_target="tpu_custom_call" | custom-call | tf_op jit(solution)/shard_map/pallas_call | solution.py:172
  42.8 0.0 copy-start.2
  42.8 0.0 copy-start.10
  42.8 0.0 copy-start.6
  42.8 1.7 %multiply_convert_fusion = (bf16[192,1024]{1,0:T(8,128)(2,1)S(1)}, f32[192,1024]{1,0:T(8,128)}) fusion(bf16[1536,192]{1,0:T(8,128)(2,1)S(1)} %bitcast.45, bf16[1536,1024]{1,0:T(8,128)(2,1)S(1)} %bitcast.47), kind=kOutput, calls=%fused_computation.18 | convolution fusion | flops 604962816 | bytes 4915200 | tf_op jit(solution)/shard_map/dot_general | solution.py:467
  44.6 0.0 copy-done.2
  44.6 0.0 copy-done.10
  44.6 0.2 convert_reduce_fusion
  44.7 0.2 fusion.3
  45.0 0.0 copy-done.6
  45.0 0.5 fusion.9
  45.5 0.0 copy-done
  45.5 0.0 copy-start.14
  45.5 0.0 copy-start.7
  45.6 0.0 copy-start.8
  45.6 0.0 copy-start.11
  45.6 1.4 %multiply_convert_fusion.1 = (bf16[160,1024]{1,0:T(8,128)(2,1)S(1)}, f32[160,1024]{1,0:T(8,128)}) fusion(f32[160,1024]{1,0:T(8,128)S(1)} %fusion.9, bf16[160,1024]{1,0:T(8,128)(2,1)S(1)} %fusion.3, bf16[1024,1024]{1,0:T(8,128)(2,1)S(1)} %copy-done), kind=kOutput, calls=%fused_computation.21 | convolution fusion | flops 336527360 | bytes 4063232 | tf_op jit(solution)/shard_map/dot_general | solution.py:428
  47.0 0.0 copy-done.14
  47.0 0.0 copy-start.9
  47.0 0.2 fusion.6
  47.3 0.0 copy-done.7
  47.3 0.3 fusion.12
  47.5 0.0 copy-done.8
  47.6 0.0 copy-done.11
  47.6 0.9 exponential_reduce_fusion
  48.4 0.0 copy-done.9
  48.4 0.1 multiply_convert_fusion.2
  48.5 1.0 fusion.20
  49.6 0.0 copy-done.12
  49.6 2.6 %fusion.4.g2 = bf16[160,1024]{1,0:T(8,128)(2,1)} fusion(bf16[128,153]{1,0:T(8,128)(2,1)S(1)} %multiply_convert_fusion.2, bf16[1024,153]{0,1:T(8,128)(2,1)} %param.21, f32[160,1024]{1,0:T(8,128)} %get-tuple-element.28, f32[128,1024]{1,0:T(8,128)} %fusion.20, bf16[128,160]{0,1:T(8,128)(2,1)} %copy-done.9), kind=kOutput, calls=%fused_computation.11 | convolution fusion | flops 83951616 | bytes 1900800 | tf_op jit(solution)/shard_map/dot_general | solution.py:444
  52.2 3.4 %fusion.21 = f32[160,1024]{1,0:T(8,128)} fusion(bf16[160,1024]{1,0:T(8,128)(2,1)} %fusion.4.g2, bf16[1024,1024]{1,0:T(8,128)(2,1)} %param.18), kind=kOutput, calls=%fused_computation.48 | convolution fusion | flops 335544320 | bytes 3080192 | tf_op jit(solution)/shard_map/dot_general | solution.py:449
  55.6 3.3 %fusion.2.g1 = bf16[192,1024]{1,0:T(8,128)(2,1)} fusion(bf16[160,1024]{1,0:T(8,128)(2,1)} %fusion.4.g2, bf16[1024,1024]{1,0:T(8,128)(2,1)S(1)} %copy-done, f32[192,1024]{1,0:T(8,128)} %get-tuple-element.26, f32[160,1024]{1,0:T(8,128)} %fusion.21, bf16[160,192]{1,0:T(8,128)(2,1)S(1)} %convert_reduce_fusion), kind=kOutput, calls=%fused_computation.7 | convolution fusion | flops 400752640 | bytes 4321280 | tf_op jit(solution)/shard_map/dot_general | solution.py:450
  58.9 0.6 pad.14.g3
  59.6 0.9 pad_maximum_fusion.1.a3
  60.5 0.9 pad_maximum_fusion.a2
  61.4 64.0 %shard_map.163.sums = bf16[2,8,16,1024]{3,2,1,0:T(8,128)(2,1)} custom-call(bf16[2,768,192]{2,1,0:T(8,128)(2,1)} %copy-done.2, bf16[2,160,1024]{2,1,0:T(8,128)(2,1)} %pad_maximum_fusion.a2, bf16[2,128,1024]{2,1,0:T(8,128)(2,1)} %pad_maximum_fusion.1.a3, bf16[192,1024]{1,0:T(8,128)(2,1)} %fusion.2.g1, bf16[160,1024]{1,0:T(8,128)(2,1)} %fusion.4.g2, ...), custom_call_target="tpu_custom_call" | custom-call | tf_op jit(solution)/shard_map/pallas_call | solution.py:364
  125.4 2.0 %shard_map.164 = (f32[48,1024]{1,0:T(8,128)}, f32[48,1024]{1,0:T(8,128)}, f32[64,1024]{1,0:T(8,128)}, f32[64,1024]{1,0:T(8,128)}, f32[64,153]{1,0:T(8,128)}, /*index=5*/f32[64,153]{1,0:T(8,128)}) custom-call(bf16[2,8,16,1024]{3,2,1,0:T(8,128)(2,1)} %shard_map.163.sums), custom_call_target="tpu_custom_call" | custom-call | tf_op jit(solution)/shard_map/pallas_call | solution.py:397
  127.4 0.0 copy-done.13
  127.4 0.0 copy-done.15
  127.4 0.6 subtract_reduce_fusion
  (9 shorter events, 0.1 us)
Async XLA Ops:
  0.6 44.9 %copy-start = (bf16[1024,1024]{1,0:T(8,128)(2,1)S(1)}, bf16[1024,1024]{1,0:T(8,128)(2,1)}, u32[]{:S(2)}) copy-start(bf16[1024,1024]{1,0:T(8,128)(2,1)} %param.19) | copy-start | bytes 6291460
  0.6 1.6 %copy-start.1 = (bf16[1,16,1024,48]{2,3,1,0:T(8,128)(2,1)S(1)}, bf16[1,16,1024,48]{2,3,1,0:T(8,128)(2,1)}, u32[]{:S(2)}) copy-start(bf16[1,16,1024,48]{2,3,1,0:T(8,128)(2,1)} %param.11) | copy-start | bytes 4718596
  2.2 0.9 copy-start.3
  3.1 0.9 copy-start.4
  4.0 0.9 copy-start.5
  42.8 1.8 %copy-start.2 = (bf16[2,768,192]{2,1,0:T(8,128)(2,1)}, bf16[2,768,192]{2,1,0:T(8,128)(2,1)S(1)}, u32[]{:S(2)}) copy-start(bf16[2,768,192]{2,1,0:T(8,128)(2,1)S(1)} %get-tuple-element.15.a1) | copy-start | bytes 1769476
  42.8 1.8 %copy-start.10 = (s32[1,1,160,5]{2,1,3,0:T(1,128)S(1)}, s32[1,1,160,5]{2,1,3,0:T(1,128)}, u32[]{:S(2)}) copy-start(s32[1,1,160,5]{2,1,3,0:T(1,128)} %param.13) | copy-start | bytes 9604
  42.8 2.2 %copy-start.6 = (bf16[1024,1024]{1,0:T(8,128)(2,1)S(1)}, bf16[1024,1024]{1,0:T(8,128)(2,1)}, u32[]{:S(2)}) copy-start(bf16[1024,1024]{1,0:T(8,128)(2,1)} %param.18) | copy-start | bytes 6291460
  45.5 1.4 %copy-start.14 = (s32[1,1,128,3]{2,1,3,0:T(1,128)S(1)}, s32[1,1,128,3]{2,1,3,0:T(1,128)}, u32[]{:S(2)}) copy-start(s32[1,1,128,3]{2,1,3,0:T(1,128)} %param.14) | copy-start | bytes 4612
  45.5 1.7 %copy-start.7 = (bf16[1024,153]{0,1:T(8,128)(2,1)S(1)}, bf16[1024,153]{0,1:T(8,128)(2,1)}, u32[]{:S(2)}) copy-start(bf16[1024,153]{0,1:T(8,128)(2,1)} %param.20) | copy-start | bytes 940036
  45.6 2.0 %copy-start.8 = (bf16[1024,153]{0,1:T(8,128)(2,1)S(1)}, bf16[1024,153]{0,1:T(8,128)(2,1)}, u32[]{:S(2)}) copy-start(bf16[1024,153]{0,1:T(8,128)(2,1)} %param.21) | copy-start | bytes 940036
  45.6 2.0 %copy-start.11 = (s32[1,1,128]{2,1,0:T(1,128)S(1)}, s32[1,1,128]{2,1,0:T(1,128)}, u32[]{:S(2)}) copy-start(s32[1,1,128]{2,1,0:T(1,128)} %param.15) | copy-start | bytes 1540
  47.0 1.4 %copy-start.9 = (bf16[128,160]{0,1:T(8,128)(2,1)}, bf16[128,160]{0,1:T(8,128)(2,1)S(1)}, u32[]{:S(2)}) copy-start(bf16[128,160]{0,1:T(8,128)(2,1)S(1)} %convert_reduce_fusion.1) | copy-start | bytes 122884
  48.4 1.1 copy-start.12
  61.4 66.1 %copy-start.13 = (f32[128]{0:T(128)S(1)}, f32[128]{0:T(128)}, u32[]{:S(2)}) copy-start(f32[128]{0:T(128)} %copy-done.12) | copy-start | bytes 1540
  61.4 66.1 %copy-start.15 = (f32[128]{0:T(128)S(1)}, f32[128]{0:T(128)}, u32[]{:S(2)}) copy-start(f32[128]{0:T(128)} %get-tuple-element.24) | copy-start | bytes 1540

commit v2 on v0

v2 whole, which is shorter than its diff:
```python
import jax
import jax.numpy as jnp
from jax import lax
from jax.experimental import pallas as pl
from jax.experimental.pallas import tpu as pltpu
from jax.sharding import PartitionSpec as P

MESH = pl.DeviceIdType.MESH
BF = jnp.bfloat16
F32 = jnp.float32
FAN1 = 5
FAN2 = 5
FAN3 = 3
R0 = 1024
R1 = 192
R2 = 160
SEEDS = 128
HID = 1024
CUTS = 16
WIDE = 48
ROWS = CUTS * WIDE
CLASSES = 153
PADDED = 256
VMEM = pl.BlockSpec(memory_space=pltpu.VMEM)
ANY = pl.BlockSpec(memory_space=pl.ANY)
SLOTS = 192
UPPER = (48, 32)
LOWER = (16, 32)


def dot(a, b):
    return jnp.dot(a, b, preferred_element_type=F32)


def dot_nt(a, b):
    return lax.dot_general(a, b, (((1,), (1,)), ((), ())), preferred_element_type=F32)


def sigmoid(v):
    return 1.0 / (1.0 + jnp.exp(-v))


def slope(v):
    s = sigmoid(v)
    return s * (1.0 + v * (1.0 - s))


def lanes(n, width=256):
    if isinstance(n, int):
        return slice(n * width, (n + 1) * width)
    return pl.ds(pl.multiple_of(n * width, width), width)


def kernel(
    lists_hbm, xt_hbm, w_self_hbm, w_neigh_hbm, second_self_hbm, second_neigh_hbm, final_hbm, third_hbm, idx,
    loss, out_a, out_b,
    lists, xt, w_in, second, raw, top,
    blk_out, blk_in, wa, wb, at,
    pre1, act1, mean2, pre2, act2, mean3, back2, g1, g2, g3,
    ra1, ra2, ra3, rg1, rg2, rg3,
    *rest,
):
    bufs_a, bufs_b = rest[:13], rest[13:26]
    rest_keep, rest_rz = rest[26:30], rest[30:32]
    load, send, recv, a_send, a_recv = rest[32:]
    d, c = lax.axis_index("dp"), lax.axis_index("cuts")
    x, y, zh, zl, k = c // 4, d // 4, c % 4, (d // 2) % 2, d % 2
    me = c

    def device(px, py, pzh, pzl, pk):
        return {"dp": (py * 2 + pzl) * 2 + pk, "cuts": px * 4 + pzh}

    def peer(dx=0, dy=0, dzh=0, dzl=0, dk=0):
        return device((x + dx) % 4, (y + dy) % 4, (zh + dzh) % 4, (zl + dzl) % 2, (k + dk) % 2)

    sibling = peer(dk=1)
    xs = [(x + s) % 4 for s in range(4)]
    ys = [(y + s) % 4 for s in range(4)]

    barrier = pltpu.get_barrier_semaphore()
    peers = [peer(dx=s // 4, dzh=s % 4) for s in range(1, 16)]
    peers += [peer(dy=s // 2, dzl=s % 2) for s in range(1, 8)]
    peers += [peer(dzh=s, dzl=1) for s in range(1, 4)]
    peers += [sibling]
    for p in peers:
        pl.semaphore_signal(barrier, 1, device_id=p, device_id_type=MESH)

    count = [0]

    def fetch(src, dst):
        cp = pltpu.make_async_copy(src, dst, load.at[count[0]])
        count[0] += 1
        cp.start()
        return cp

    ld_lists = fetch(lists_hbm, lists)
    ld_w = [fetch(w_self_hbm, w_in.at[0]), fetch(w_neigh_hbm, w_in.at[1])]

    def xt_copy(s):
        m = (me + s) % CUTS
        return pltpu.make_async_copy(xt_hbm.at[m], xt.at[m], load.at[16 + s])

    def xt_start(s, _):
        xt_copy(s).start()
        return 0

    lax.fori_loop(1, CUTS + 1, xt_start, 0)
    ld_top = [fetch(final_hbm, raw.at[0]), fetch(third_hbm, raw.at[1])]
    ld_second = [fetch(second_self_hbm, second.at[0]), fetch(second_neigh_hbm, second.at[1])]

    sends = []

    def link(src, dst, to):
        n = len(sends)
        cp = pltpu.make_async_remote_copy(
            src_ref=src, dst_ref=dst, send_sem=send.at[n], recv_sem=recv.at[n], device_id=to, device_id_type=MESH
        )
        cp.start()
        sends.append(cp)
        return n

    def arrived(n, dst):
        pltpu.make_async_remote_copy(
            src_ref=dst, dst_ref=dst, send_sem=send.at[n], recv_sem=recv.at[n], device_id=sibling, device_id_type=MESH
        ).wait_recv()

    for cp in ld_w:
        cp.wait()
    for kk in range(2):
        wa[kk, me] = w_in[kk, :, 0:512]
    wb[k, y, me] = w_in[k, :, pl.ds(pl.multiple_of(512 + y * 128, 128), 128)]
    ld_lists.wait()
    pl.semaphore_wait(barrier, len(peers))

    wz = [
        (link(wa.at[k, me], wa.at[k, me], peer(dzh=s)), link(wb.at[k, y, me], wb.at[k, y, me], peer(dzh=s)))
        for s in range(1, 4)
    ]

    def spread_x(j):
        src = x * 4 + (zh + 4 - j) % 4
        return [link(wa.at[k, src], wa.at[k, src], peer(dx=s)) for s in range(1, 4)]

    wx = {0: spread_x(0)}
    wk = {}

    def spread_core(key, src):
        wk[key] = link(wa.at[k, src], wa.at[k, src], sibling)

    def block(m):
        rows = lax.broadcasted_iota(jnp.int32, (R0, R1), 0)
        counts = jnp.zeros((R0, R1), F32)
        for f in range(FAN1):
            counts = counts + jnp.where(rows == lists[f, pl.ds(m, 1), :], 1.0, 0.0)
        mean = (dot(xt[m], counts.astype(BF)) * (1.0 / FAN1)).astype(BF)
        return xt[m][:, :R1], mean

    def pack(ref, m, own, mean):
        ref[m, 0:48] = own[:, 0:128]
        ref[m, 48:96] = mean[:, 0:128]
        ref[m, 96:144] = jnp.concatenate([own[:, 128:192], mean[:, 128:192]], axis=1)

    def a_copy(s):
        m = (me + s) % CUTS
        return pltpu.make_async_remote_copy(
            src_ref=blk_out.at[m], dst_ref=blk_in.at[me], send_sem=a_send.at[s - 1], recv_sem=a_recv.at[s - 1],
            device_id={"dp": d, "cuts": m}, device_id_type=MESH,
        )

    def one(s, _):
        m = (me + s) % CUTS
        xt_copy(s).wait()
        own, mean = block(m)
        pack(blk_out, m, own, mean)
        a_copy(s).start()
        return 0

    def z_arrival(j):
        src = x * 4 + (zh + 4 - j) % 4
        arrived(wz[j - 1][0], wa.at[k, src])
        arrived(wz[j - 1][1], wb.at[k, y, src])
        wx[j] = spread_x(j)

    def mine_x(dx):
        return pl.ds(pl.multiple_of(((x + 4 + dx) % 4) * 4, 4), 4)

    lax.fori_loop(1, 5, one, 0)
    for j in (1, 3, 2):
        z_arrival(j)
    wbx = [link(wb.at[k, y, mine_x(0)], wb.at[k, y, mine_x(0)], peer(dx=s)) for s in range(1, 4)]
    for j in (1, 3, 2):
        spread_core((j, 0), x * 4 + (zh + 4 - j) % 4)
    lax.fori_loop(5, 10, one, 0)
    for s in range(1, 4):
        arrived(wbx[s - 1], wb.at[k, y, mine_x(-s)])
    wby = [link(wb.at[k, y], wb.at[k, y], peer(dy=s)) for s in range(1, 4)]
    wbk = {0: link(wb.at[k, y], wb.at[k, y], sibling)}
    lax.fori_loop(10, 16, one, 0)
    xt_copy(16).wait()
    own, mean = block(me)
    pack(blk_in, me, own, mean)

    for cp in ld_top:
        cp.wait()
    for i in range(2):
        top[i, 144:256] = jnp.zeros((112, HID), BF)
        top[i, 0:CLASSES] = raw[i]
    rows256 = lax.broadcasted_iota(jnp.int32, (256, 256), 0)

    def counting(first, fan):
        counts = jnp.zeros((256, 256), F32)
        for f in range(first, first + fan):
            counts = counts + jnp.where(rows256 == idx[f:f + 1, :], 1.0, 0.0)
        return counts

    counts2t, counts3t = counting(0, FAN2), counting(FAN2, FAN3)
    counts2, counts3 = counts2t.T.astype(BF), counts3t.T.astype(BF)
    counts2t, counts3t = counts2t.astype(BF), counts3t.astype(BF)
    onehot = jnp.where(rows256 == idx[8:9, :], 1.0, 0.0).T[:SEEDS]
    act1[R1:256] = jnp.zeros((256 - R1, HID), BF)
    act2[R2:256] = jnp.zeros((256 - R2, HID), BF)
    back2[R2:256] = jnp.zeros((256 - R2, HID), BF)

    for j in (0, 1, 3, 2):
        for s in range(1, 4):
            src = ((x + 4 - s) % 4) * 4 + (zh + 4 - j) % 4
            arrived(wx[j][s - 1], wa.at[k, src])
            spread_core((j, s), src)
    for s in range(1, CUTS):
        frm = (me + CUTS - s) % CUTS
        pltpu.make_async_remote_copy(
            src_ref=blk_in.at[frm], dst_ref=blk_in.at[frm], send_sem=a_send.at[s - 1], recv_sem=a_recv.at[s - 1],
            device_id=sibling, device_id_type=MESH,
        ).wait_recv()
    for i in range(CUTS):
        tail = blk_in[i, 96:144]
        at[0, i * 48:(i + 1) * 48, 0:128] = blk_in[i, 0:48]
        at[1, i * 48:(i + 1) * 48, 0:128] = blk_in[i, 48:96]
        at[0, i * 48:(i + 1) * 48, 128:192] = tail[:, 0:64]
        at[1, i * 48:(i + 1) * 48, 128:192] = tail[:, 64:128]
    sw_a1 = link(at.at[1 - k], ra1, sibling)
    at0, at1 = at[0].T, at[1].T
    for s in range(1, 4):
        frm = (y + 4 - s) % 4
        arrived(wby[s - 1], wb.at[k, frm])
        wbk[s] = link(wb.at[k, frm], wb.at[k, frm], sibling)
    for (j, s), n in wk.items():
        arrived(n, wa.at[1 - k, ((x + 4 - s) % 4) * 4 + (zh + 4 - j) % 4])
    for s in range(4):
        arrived(wbk[s], wb.at[1 - k, (y + 4 - s) % 4])

    for n in range(4):
        if n < 2:
            w0, w1 = (wa[i, :, :, lanes(n)].reshape(ROWS, 256) for i in range(2))
        else:
            q = 2 * n - 4
            w0, w1 = (
                jnp.concatenate([wb[i, q].reshape(ROWS, 128), wb[i, q + 1].reshape(ROWS, 128)], axis=1)
                for i in range(2)
            )
        v = dot(at0, w0) + dot(at1, w1)
        pre1[:, lanes(n)] = v
        act1[0:R1, lanes(n)] = (v * sigmoid(v)).astype(BF)
    for n in range(4):
        mean2[:, lanes(n)] = (dot(counts2[:R2], act1[:, lanes(n)]) * (1.0 / FAN2)).astype(BF)
    for cp in ld_second:
        cp.wait()
    for n in range(4):
        v = dot(act1[0:R2], second[0, :, lanes(n)]) + dot(mean2[...], second[1, :, lanes(n)])
        pre2[:, lanes(n)] = v
        act2[0:R2, lanes(n)] = (v * sigmoid(v)).astype(BF)
    for n in range(4):
        mean3[:, lanes(n)] = (dot(counts3[:SEEDS], act2[:, lanes(n)]) * (1.0 / FAN3)).astype(BF)
    logits = dot_nt(act2[0:SEEDS], top[0]) + dot_nt(mean3[...], top[1])
    column = lax.broadcasted_iota(jnp.int32, (SEEDS, PADDED), 1)
    expon = jnp.where(column < CLASSES, jnp.exp(logits), 0.0)
    total = jnp.sum(expon, axis=1, keepdims=True)
    each = jnp.log(total) - jnp.sum(logits * onehot, axis=1, keepdims=True)
    loss[...] = jnp.sum(each, axis=0, keepdims=True) * (1.0 / SEEDS)
    g3[...] = ((expon / total - onehot) * (1.0 / SEEDS)).astype(BF)

    sw_g3 = link(g3, rg3, sibling)
    keep3, keep2, give3, give2 = rest_keep
    give3[...] = jnp.where(k == 0, mean3[...], act2[0:SEEDS])
    keep3[...] = jnp.where(k == 0, act2[0:SEEDS], mean3[...])
    sw_a3 = link(give3, ra3, sibling)
    give2[...] = jnp.where(k == 0, mean2[...], act1[0:R2])
    keep2[...] = jnp.where(k == 0, act1[0:R2], mean2[...])
    sw_a2 = link(give2, ra2, sibling)
    for n in range(4):
        back = (dot(g3[...], top[1, :, lanes(n)]) * (1.0 / FAN3)).astype(BF)
        own = dot(g3[...], top[0, :, lanes(n)])
        grad = dot(counts3t[:R2, :SEEDS], back) + jnp.concatenate([own, jnp.zeros((R2 - SEEDS, 256), F32)], axis=0)
        g2[:, lanes(n)] = (grad * slope(pre2[:, lanes(n)])).astype(BF)
    sw_g2 = link(g2, rg2, sibling)

    class Ring:
        def __init__(self, block, add, up, down, relay, direct, comb):
            self.block, self.add, self.up, self.down = block, add, up, down
            self.relay, self.direct, self.comb = relay, direct, comb

        def opposite(self):
            self.n_relay = (
                link(self.block(2, 0), self.relay.at[0], self.up), link(self.block(2, 1), self.relay.at[1], self.down)
            )

        def to_up(self):
            self.n_up = link(self.block(1, 1), self.direct.at[1], self.up)

        def to_down(self):
            self.n_down = link(self.block(3, 0), self.direct.at[0], self.down)

        def pass_on(self):
            self.n_comb = []
            for h, off, to in ((0, 1, self.up), (1, 3, self.down)):
                arrived(self.n_relay[h], self.relay.at[h])
                self.add(self.relay.at[h], (self.relay.at[h], self.block(off, h)))
                self.n_comb.append(link(self.relay.at[h], self.comb.at[h], to))

        def finish(self, out):
            for h, n in ((0, self.n_down), (1, self.n_up)):
                arrived(self.n_comb[h], self.comb.at[h])
                arrived(n, self.direct.at[h])
                self.add(out(h), (self.block(0, h), self.comb.at[h], self.direct.at[h]))

    def add_leading(dst, parts):
        def body(i, _):
            v = parts[0][i].astype(F32)
            for p in parts[1:]:
                v = v + p[i].astype(F32)
            dst[i] = v.astype(BF)
            return 0

        lax.fori_loop(0, dst.shape[0], body, 0)

    class Chunk:
        def __init__(self, sizes, bufs, out):
            self.rows, self.out = sizes, out
            (
                self.s1, self.s2, rel1, dir1, com1, rel2, dir2, com2, self.t1, self.t2, self.q1, self.q2, self.u,
            ) = bufs[:13]
            self.y = Ring(
                lambda off, h: self.s1.at[ys[off], pl.ds(8 * h, 8)], add_leading, peer(dy=1), peer(dy=3), rel1, dir1, com1
            )
            self.x = Ring(
                lambda off, h: self.s2.at[:, pl.ds(xs[off] * 4 + 2 * h, 2)],
                add_leading, peer(dx=1), peer(dx=3), rel2, dir2, com2,
            )

        def first_done(self):
            self.y.finish(lambda h: self.t1.at[pl.ds(8 * h, 8)])
            self.n1 = [link(self.t1.at[mine_x(s)], self.q1.at[s - 1], peer(dx=s)) for s in range(1, 4)]
            self.x.finish(lambda h: self.t2.at[:, pl.ds(2 * h, 2)])
            self.n2 = [link(self.t2.at[ys[s]], self.q2.at[s - 1], peer(dy=s)) for s in range(1, 4)]

        def second_done(self, rz):
            r1, r2 = self.rows
            for lo, hi, numbers, t, q in (
                (0, r1, self.n1, lambda h: self.t1[x * 4 + h], self.q1),
                (r1, r1 + r2, self.n2, lambda h: self.t2[y, h], self.q2),
            ):
                for s in range(3):
                    arrived(numbers[s], q.at[s])
                for h in range(4):
                    v = t(h).astype(F32)
                    for s in range(3):
                        v = v + q[s, h].astype(F32)
                    v = v.astype(BF)
                    self.u[0, h, lo:hi] = v[:, 0:128]
                    self.u[1, h, lo:hi] = v[:, 128:256]
            self.rz = rz
            self.n3 = []
            for s in range(1, 8):
                p = (zl * 4 + zh + s) % 8
                self.n3.append(link(self.u.at[p // 4, p % 4], rz.at[s - 1], device(x, y, p % 4, p // 4, k)))

        def third_done(self):
            v = self.u[zl, zh].astype(F32)
            for s in range(7):
                arrived(self.n3[s], self.rz.at[s])
                v = v + self.rz[s].astype(F32)
            self.mine = y * 2 + zl
            piece = self.out.at[k, self.mine]
            self.out[k, self.mine] = v.astype(BF)
            self.n4 = []
            for s in range(1, 8):
                p = (self.mine + s) % 8
                self.n4.append(link(piece, piece, device(x, p // 2, zh, p % 2, k)))

        def gathered(self):
            for s in range(1, 8):
                arrived(self.n4[s - 1], self.out.at[k, (self.mine + 8 - s) % 8])
            self.n5 = link(self.out.at[k], self.out.at[k], sibling)

        def done(self):
            arrived(self.n5, self.out.at[1 - k])

    upper, lower = Chunk(UPPER, bufs_a, out_a), Chunk(LOWER, bufs_b, out_b)
    order = (2, 1, 3, 0)

    arrived(sw_g3, rg3)
    arrived(sw_a3, ra3)
    third = (dot(keep3[...].T, g3[...]) + dot(ra3[...].T, rg3[...])).astype(BF).reshape(CUTS, 4, 16, 256)
    for j in range(4):
        upper.s2[j, :, 16:32] = third[:, j]
    keep_t = keep2[...].T
    arrived(sw_a2, ra2)
    sib_t = ra2[...].T
    arrived(sw_g2, rg2)
    for off in order:
        n = ys[off]
        p = (dot(keep_t, g2[:, lanes(n)]) + dot(sib_t, rg2[:, lanes(n)])).astype(BF).reshape(CUTS, 64, 256)
        upper.s1[n] = p[:, 0:48]
        upper.s2[n, :, 0:16] = p[:, 48:64]
        if off == 2:
            upper.y.opposite()
        if off == 1:
            upper.y.to_up()
        if off == 3:
            upper.y.to_down()
    upper.x.opposite()
    upper.x.to_up()
    upper.x.to_down()

    for n in range(4):
        back2[0:R2, lanes(n)] = (dot_nt(g2[...], second[1, lanes(n), :]) * (1.0 / FAN2)).astype(BF)
    for n in range(4):
        own = dot_nt(g2[...], second[0, lanes(n), :])
        grad = dot(counts2t[:R1], back2[:, lanes(n)]) + jnp.concatenate(
            [own, jnp.zeros((R1 - R2, 256), F32)], axis=0
        )
        g1[:, lanes(n)] = (grad * slope(pre1[:, lanes(n)])).astype(BF)
    sw_g1 = link(g1, rg1, sibling)
    upper.y.pass_on()
    arrived(sw_a1, ra1)
    arrived(sw_g1, rg1)
    for off in order:
        n = ys[off]
        p = (dot(at[k], g1[:, lanes(n)]) + dot(ra1[...], rg1[:, lanes(n)])).astype(BF).reshape(CUTS, 48, 256)
        lower.s1[n] = p[:, 0:16]
        lower.s2[n] = p[:, 16:48]
        if off == 2:
            lower.y.opposite()
        if off == 1:
            lower.y.to_up()
            upper.x.pass_on()
        if off == 3:
            lower.y.to_down()
    lower.x.opposite()
    lower.x.to_up()
    lower.x.to_down()
    upper.first_done()
    lower.y.pass_on()
    lower.x.pass_on()
    upper.second_done(rest_rz[0])
    lower.first_done()
    upper.third_done()
    lower.second_done(rest_rz[1])
    upper.gathered()
    lower.third_done()
    lower.gathered()
    upper.done()
    lower.done()

    for cp in sends:
        cp.wait_send()

    def sent(s, _):
        a_copy(s).wait_send()
        return 0

    lax.fori_loop(1, CUTS, sent, 0)


def step(lists, xt, w_self, w_neigh, second_self, second_neigh, final_t, third_t, idx):
    dma = pltpu.SemaphoreType.DMA
    vm = lambda *shape: pltpu.VMEM(shape, BF)
    vf = lambda *shape: pltpu.VMEM(shape, F32)

    def chunk(sizes):
        r1, r2 = sizes
        return [
            vm(4, CUTS, r1, 256), vm(4, CUTS, r2, 256),
            vm(2, 8, r1, 256), vm(2, 8, r1, 256), vm(2, 8, r1, 256),
            vm(2, 4, 2, r2, 256), vm(2, 4, 2, r2, 256), vm(2, 4, 2, r2, 256),
            vm(CUTS, r1, 256), vm(4, 4, r2, 256),
            vm(3, 4, r1, 256), vm(3, 4, r2, 256),
            vm(2, 4, r1 + r2, 128),
        ]

    return pl.pallas_call(
        kernel,
        out_shape=(
            jax.ShapeDtypeStruct((1, 1), F32),
            jax.ShapeDtypeStruct((2, 8, sum(UPPER), 128), BF),
            jax.ShapeDtypeStruct((2, 8, sum(LOWER), 128), BF),
        ),
        in_specs=[ANY] * 8 + [VMEM],
        out_specs=(VMEM,) * 3,
        scratch_shapes=[
            pltpu.VMEM((FAN1, CUTS, R1), jnp.int32), vm(CUTS, WIDE, R0), vm(2, WIDE, HID), vm(2, HID, HID),
            vm(2, CLASSES, HID), vm(2, PADDED, HID),
            vm(CUTS, 144, 128), vm(CUTS, 144, 128), vm(2, CUTS, WIDE, 512), vm(2, 4, CUTS, WIDE, 128), vm(2, ROWS, R1),
            vf(R1, HID), vm(256, HID), vm(R2, HID), vf(R2, HID), vm(256, HID), vm(SEEDS, HID), vm(256, HID),
            vm(R1, HID), vm(R2, HID), vm(SEEDS, PADDED),
            vm(ROWS, R1), vm(R2, HID), vm(SEEDS, HID), vm(R1, HID), vm(R2, HID), vm(SEEDS, PADDED),
        ]
        + chunk(UPPER)
        + chunk(LOWER)
        + [
            vm(SEEDS, HID), vm(R2, HID), vm(SEEDS, HID), vm(R2, HID),
            vm(7, sum(UPPER), 128), vm(7, sum(LOWER), 128),
            dma((40,)), dma((SLOTS,)), dma((SLOTS,)), dma((15,)), dma((15,)),
        ],
        compiler_params=pltpu.CompilerParams(
            collective_id=1, has_side_effects=True, vmem_limit_bytes=56 * 2**20
        ),
    )(lists, xt, w_self, w_neigh, second_self, second_neigh, final_t, third_t, idx)


def finish_kernel(upper, lower, first_self, first_neigh, second_self, second_neigh, third_self, third_neigh):
    for k, first, second, third in (
        (0, first_self, second_self, third_self), (1, first_neigh, second_neigh, third_neigh)
    ):
        for g in range(8):
            first[:, lanes(g, 128)] = lower[k, g].astype(F32)
            second[:, lanes(g, 128)] = upper[k, g, 0:64].astype(F32)
            lo = (g % 2) * 128
            width = min(128, CLASSES - lo)
            third[g // 2 * 16:g // 2 * 16 + 16, lo:lo + width] = upper[k, g, 64:80, 0:width].astype(F32)


def finish(upper, lower):
    shapes = ((48, HID), (48, HID), (64, HID), (64, HID), (64, CLASSES), (64, CLASSES))
    return pl.pallas_call(
        finish_kernel,
        out_shape=tuple(jax.ShapeDtypeStruct(s, F32) for s in shapes),
        in_specs=[VMEM] * 2,
        out_specs=(VMEM,) * 6,
    )(upper, lower)


def per_device(
    features, lists_one, lists_two, lists_three, labels, initial_node_weight, initial_neighbour_weight,
    second_self, second_neigh, final_node_weight, third_neigh,
):
    xt = jnp.swapaxes(features[0], 1, 2)
    lists = jnp.transpose(lists_one[0], (2, 0, 1))

    def padded(v):
        return jnp.pad(v, ((0, 0), (0, 256 - v.shape[1])), constant_values=-1)

    idx = jnp.concatenate(
        [padded(lists_two[0, 0].T), padded(lists_three[0, 0].T), padded(labels[0]), jnp.full((7, 256), -1, jnp.int32)]
    )
    loss, upper, lower = step(
        lists, xt, initial_node_weight, initial_neighbour_weight, second_self, second_neigh,
        final_node_weight.T, third_neigh.T, idx,
    )
    return (loss,) + tuple(finish(upper, lower))


def solution(mesh):
    return jax.shard_map(
        per_device,
        mesh=mesh,
        in_specs=(
            P("dp", None, None, "cuts"),
            P("dp", None, None, None),
            P("dp", "cuts", None, None),
            P("dp", "cuts", None, None),
            P("dp", "cuts", None),
            P("cuts", None),
            P("cuts", None),
            P(), P(), P(), P(),
        ),
        out_specs=(P("dp", "cuts"),) + (P("cuts", None),) * 6,
        check_vma=False,
    )
```

time: 810 us -> 105 us (0.13)
  waiting for transfers between devices: 663 us -> 0 us
  Pallas kernels: 0 us -> 100 us
  matrix products: 57.2 us -> 0 us
  blocking collectives: 52.1 us -> 0 us
  other arithmetic: 17.6 us -> 1.33 us
  between operations: 16.1 us -> 2.42 us
    reduce_scatter x5 -> x0, waiting for transfers between devices: 513 us -> none  [the longest x1 164 us: per_device(): lax.psum_scatter(jnp.einsum('cnk,ke->cne', node_own_term, initial_node_we...]
    pallas_call x0 -> x2, Pallas kernels: none -> 100 us  [the longest x1 98 us: step(): pl.pallas_call(kernel, out_shape=(jax.ShapeDtypeStruct((1, 1), F32), jax....]
    all_gather x1 -> x0, waiting for transfers between devices: 81.4 us -> none  [per_device(): lax.all_gather(grad_pre_one[None], 'cuts', axis=0, tiled=True)]
    psum x1 -> x0, waiting for transfers between devices: 69.3 us -> none  [per_device(): lax.psum(group_self.astype(jnp.bfloat16), 'dp').astype(jnp.float32)]
    dot_general x34 -> x0, matrix products: 57.2 us -> none  [the longest x18 18.7 us: aggregate(): summed = jnp.dot(counts, source, preferred_element_type=jnp.float32)]
    psum x1 -> x0, blocking collectives: 52.1 us -> none  [per_device(): lax.psum(sliced[2].astype(jnp.bfloat16), 'dp').astype(jnp.float32)]
    convert_element_type x8 -> x0, other arithmetic: 9.06 us -> none  [the longest x1 1.62 us: per_device(): lax.psum(sliced[1].astype(jnp.bfloat16), 'dp').astype(jnp.float32)]
    reduce_sum x19 -> x0, other arithmetic: 8.53 us -> none  [the longest x18 7.92 us: counting(): return jnp.sum(hits.astype(jnp.float32), axis=1).astype(jnp.bfloat16)]
  transfers between devices with their start and end apart: 7 -> 0, of which waited for: 7 -> 0; matrix products, arithmetic and copies ran while one was open for 2% -> 0% of each run, Pallas kernels for 0% -> 0%
where the time goes in v2:
time: 105 us
  Pallas kernels  100 us (95%)
  between operations  2.42 us (2%)
  local copies, waits for them, and re-layouts  1.45 us (1%)
  other arithmetic  1.33 us (1%)
    pallas_call x1, Pallas kernels, step(): pl.pallas_call(kernel, out_shape=(jax.ShapeDtypeStruct((1, 1), F32), jax....  98 us

profile of v2, /device:TPU:1, one launch (start us, length us, event | category | flops | bytes accessed | tf_op | source)
XLA Modules:
  0.0 105.2 jit_solution(16399604418014879241)
XLA Ops:
  0.6 0.1 pad.18.clone
  0.7 0.7 copy.23
  1.4 0.7 copy.22
  2.1 1.3 %fusion.idx = s32[16,256]{1,0:T(8,128)} fusion(s32[1,128]{1,0:T(1,128)} %bitcast.25, s32[3,128]{1,0:T(4,128)S(1)} %bitcast.24, s32[5,160]{1,0:T(8,128)S(1)} %bitcast.23, s32[16]{0:T(128)S(1)} %pad.18.clone), kind=kLoop, calls=%fused_computation.5 | loop fusion | flops 53248 | bytes 21696 | tf_op jit(solution)/shard_map/concatenate | solution.py:553
  3.4 98.0 %shard_map.162 = (f32[1,1]{1,0:T(1,128)}, bf16[2,8,80,128]{3,2,1,0:T(8,128)(2,1)}, bf16[2,8,48,128]{3,2,1,0:T(8,128)(2,1)}) custom-call(s32[5,16,192]{2,1,0:T(8,128)} %bitcast.22, bf16[16,48,1024]{2,1,0:T(8,128)(2,1)} %bitcast.19, bf16[48,1024]{1,0:T(8,128)(2,1)} %w_self_hbm.1, bf16[48,1024]{1,0:T(8,128)(2,1)} %w_neigh_hbm.1, ...), custom_call_target="tpu_custom_call" | custom-call | tf_op jit(solution)/shard_map/pallas_call | solution.py:491
  101.4 2.0 %shard_map.163 = (f32[48,1024]{1,0:T(8,128)}, f32[48,1024]{1,0:T(8,128)}, f32[64,1024]{1,0:T(8,128)}, f32[64,1024]{1,0:T(8,128)}, f32[64,153]{1,0:T(8,128)}, /*index=5*/f32[64,153]{1,0:T(8,128)}) custom-call(bf16[2,8,80,128]{3,2,1,0:T(8,128)(2,1)} %get-tuple-element.17.upper, bf16[2,8,48,128]{3,2,1,0:T(8,128)(2,1)} %get-tuple-element.18.lower), custom_call_target="tpu_custom_call" | custom-call | tf_op jit(solution)/shard_map/pallas_call | solution.py:535
  (1 shorter events, 0.0 us)

commit v3 on v2

--- a/solution.py
+++ b/solution.py
@@ -52,9 +52,10 @@
 
 
 def kernel(
-    lists_hbm, xt_hbm, w_self_hbm, w_neigh_hbm, second_self_hbm, second_neigh_hbm, final_hbm, third_hbm, idx,
+    lists_hbm, xt_hbm, w_self_hbm, w_neigh_hbm, second_self_hbm, second_neigh_hbm, final_hbm, third_hbm,
+    lists2_hbm, lists3_hbm, labels_hbm,
     loss, out_a, out_b,
-    lists, xt, w_in, second, raw, top,
+    lists, lists2, lists3, labels, idx, xt, w_in, second, raw, top,
     blk_out, blk_in, wa, wb, at,
     pre1, act1, mean2, pre2, act2, mean3, back2, g1, g2, g3,
     ra1, ra2, ra3, rg1, rg2, rg3,
@@ -94,6 +95,7 @@
         return cp
 
     ld_lists = fetch(lists_hbm, lists)
+    ld_idx = [fetch(lists2_hbm, lists2), fetch(lists3_hbm, lists3), fetch(labels_hbm, labels)]
     ld_w = [fetch(w_self_hbm, w_in.at[0]), fetch(w_neigh_hbm, w_in.at[1])]
 
     def xt_copy(s):
@@ -132,10 +134,8 @@
     ld_lists.wait()
     pl.semaphore_wait(barrier, len(peers))
 
-    wz = [
-        (link(wa.at[k, me], wa.at[k, me], peer(dzh=s)), link(wb.at[k, y, me], wb.at[k, y, me], peer(dzh=s)))
-        for s in range(1, 4)
-    ]
+    wbz = [link(wb.at[k, y, me], wb.at[k, y, me], peer(dzh=s)) for s in range(1, 4)]
+    waz = [link(wa.at[k, me], wa.at[k, me], peer(dzh=s)) for s in range(1, 4)]
 
     def spread_x(j):
         src = x * 4 + (zh + 4 - j) % 4
@@ -148,11 +148,17 @@
         wk[key] = link(wa.at[k, src], wa.at[k, src], sibling)
 
     def block(m):
-        rows = lax.broadcasted_iota(jnp.int32, (R0, R1), 0)
-        counts = jnp.zeros((R0, R1), F32)
-        for f in range(FAN1):
-            counts = counts + jnp.where(rows == lists[f, pl.ds(m, 1), :], 1.0, 0.0)
-        mean = (dot(xt[m], counts.astype(BF)) * (1.0 / FAN1)).astype(BF)
+        one, zero = jnp.ones((16, R1), BF), jnp.zeros((16, R1), BF)
+        wanted = [jnp.broadcast_to(lists[f, pl.ds(m, 1), :], (16, R1)).astype(jnp.int16) for f in range(FAN1)]
+        base = lax.broadcasted_iota(jnp.int32, (16, R1), 0).astype(jnp.int16)
+        parts = []
+        for b in range(R0 // 16):
+            row = base + jnp.int16(16 * b)
+            v = jnp.where(row == wanted[0], one, zero)
+            for f in range(1, FAN1):
+                v = v + jnp.where(row == wanted[f], one, zero)
+            parts.append(v)
+        mean = (dot(xt[m], jnp.concatenate(parts, axis=0)) * (1.0 / FAN1)).astype(BF)
         return xt[m][:, :R1], mean
 
     def pack(ref, m, own, mean):
@@ -175,27 +181,30 @@
         a_copy(s).start()
         return 0
 
+    def behind(j):
+        return x * 4 + (zh + 4 - j) % 4
+
     def z_arrival(j):
-        src = x * 4 + (zh + 4 - j) % 4
-        arrived(wz[j - 1][0], wa.at[k, src])
-        arrived(wz[j - 1][1], wb.at[k, y, src])
+        arrived(waz[j - 1], wa.at[k, behind(j)])
         wx[j] = spread_x(j)
+        spread_core((j, 0), behind(j))
 
     def mine_x(dx):
         return pl.ds(pl.multiple_of(((x + 4 + dx) % 4) * 4, 4), 4)
 
     lax.fori_loop(1, 5, one, 0)
-    for j in (1, 3, 2):
-        z_arrival(j)
+    for j in range(1, 4):
+        arrived(wbz[j - 1], wb.at[k, y, behind(j)])
     wbx = [link(wb.at[k, y, mine_x(0)], wb.at[k, y, mine_x(0)], peer(dx=s)) for s in range(1, 4)]
-    for j in (1, 3, 2):
-        spread_core((j, 0), x * 4 + (zh + 4 - j) % 4)
-    lax.fori_loop(5, 10, one, 0)
+    lax.fori_loop(5, 8, one, 0)
+    z_arrival(1)
+    z_arrival(3)
     for s in range(1, 4):
         arrived(wbx[s - 1], wb.at[k, y, mine_x(-s)])
     wby = [link(wb.at[k, y], wb.at[k, y], peer(dy=s)) for s in range(1, 4)]
     wbk = {0: link(wb.at[k, y], wb.at[k, y], sibling)}
-    lax.fori_loop(10, 16, one, 0)
+    z_arrival(2)
+    lax.fori_loop(8, 16, one, 0)
     xt_copy(16).wait()
     own, mean = block(me)
     pack(blk_in, me, own, mean)
@@ -205,6 +214,14 @@
     for i in range(2):
         top[i, 144:256] = jnp.zeros((112, HID), BF)
         top[i, 0:CLASSES] = raw[i]
+    for cp in ld_idx:
+        cp.wait()
+    idx[...] = jnp.full((16, 256), -1, jnp.int32)
+    for f in range(FAN2):
+        idx[f:f + 1, 0:R2] = lists2[f]
+    for f in range(FAN3):
+        idx[FAN2 + f:FAN2 + f + 1, 0:SEEDS] = lists3[f]
+    idx[8:9, 0:SEEDS] = labels[...]
     rows256 = lax.broadcasted_iota(jnp.int32, (256, 256), 0)
 
     def counting(first, fan):
@@ -244,12 +261,14 @@
         frm = (y + 4 - s) % 4
         arrived(wby[s - 1], wb.at[k, frm])
         wbk[s] = link(wb.at[k, frm], wb.at[k, frm], sibling)
-    for (j, s), n in wk.items():
-        arrived(n, wa.at[1 - k, ((x + 4 - s) % 4) * 4 + (zh + 4 - j) % 4])
-    for s in range(4):
-        arrived(wbk[s], wb.at[1 - k, (y + 4 - s) % 4])
 
     for n in range(4):
+        if n == 0:
+            for (j, s), number in wk.items():
+                arrived(number, wa.at[1 - k, ((x + 4 - s) % 4) * 4 + (zh + 4 - j) % 4])
+        if n == 2:
+            for s in range(4):
+                arrived(wbk[s], wb.at[1 - k, (y + 4 - s) % 4])
         if n < 2:
             w0, w1 = (wa[i, :, :, lanes(n)].reshape(ROWS, 256) for i in range(2))
         else:
@@ -347,9 +366,11 @@
                 add_leading, peer(dx=1), peer(dx=3), rel2, dir2, com2,
             )
 
-        def first_done(self):
+        def first_y_done(self):
             self.y.finish(lambda h: self.t1.at[pl.ds(8 * h, 8)])
             self.n1 = [link(self.t1.at[mine_x(s)], self.q1.at[s - 1], peer(dx=s)) for s in range(1, 4)]
+
+        def first_x_done(self):
             self.x.finish(lambda h: self.t2.at[:, pl.ds(2 * h, 2)])
             self.n2 = [link(self.t2.at[ys[s]], self.q2.at[s - 1], peer(dy=s)) for s in range(1, 4)]
 
@@ -386,14 +407,17 @@
             for s in range(1, 8):
                 p = (self.mine + s) % 8
                 self.n4.append(link(piece, piece, device(x, p // 2, zh, p % 2, k)))
+            self.n5 = [link(piece, piece, sibling)]
 
         def gathered(self):
             for s in range(1, 8):
-                arrived(self.n4[s - 1], self.out.at[k, (self.mine + 8 - s) % 8])
-            self.n5 = link(self.out.at[k], self.out.at[k], sibling)
+                piece = self.out.at[k, (self.mine + 8 - s) % 8]
+                arrived(self.n4[s - 1], piece)
+                self.n5.append(link(piece, piece, sibling))
 
         def done(self):
-            arrived(self.n5, self.out.at[1 - k])
+            for s in range(8):
+                arrived(self.n5[s], self.out.at[1 - k, (self.mine + 8 - s) % 8])
 
     upper, lower = Chunk(UPPER, bufs_a, out_a), Chunk(LOWER, bufs_b, out_b)
     order = (2, 1, 3, 0)
@@ -449,11 +473,13 @@
     lower.x.opposite()
     lower.x.to_up()
     lower.x.to_down()
-    upper.first_done()
+    upper.first_y_done()
     lower.y.pass_on()
+    upper.first_x_done()
     lower.x.pass_on()
     upper.second_done(rest_rz[0])
-    lower.first_done()
+    lower.first_y_done()
+    lower.first_x_done()
     upper.third_done()
     lower.second_done(rest_rz[1])
     upper.gathered()
@@ -472,10 +498,11 @@
     lax.fori_loop(1, CUTS, sent, 0)
 
 
-def step(lists, xt, w_self, w_neigh, second_self, second_neigh, final_t, third_t, idx):
+def step(*operands):
     dma = pltpu.SemaphoreType.DMA
     vm = lambda *shape: pltpu.VMEM(shape, BF)
     vf = lambda *shape: pltpu.VMEM(shape, F32)
+    vi = lambda *shape: pltpu.VMEM(shape, jnp.int32)
 
     def chunk(sizes):
         r1, r2 = sizes
@@ -495,10 +522,10 @@
             jax.ShapeDtypeStruct((2, 8, sum(UPPER), 128), BF),
             jax.ShapeDtypeStruct((2, 8, sum(LOWER), 128), BF),
         ),
-        in_specs=[ANY] * 8 + [VMEM],
+        in_specs=[ANY] * 11,
         out_specs=(VMEM,) * 3,
         scratch_shapes=[
-            pltpu.VMEM((FAN1, CUTS, R1), jnp.int32), vm(CUTS, WIDE, R0), vm(2, WIDE, HID), vm(2, HID, HID),
+            vi(FAN1, CUTS, R1), vi(FAN2, 1, R2), vi(FAN3, 1, SEEDS), vi(1, SEEDS), vi(16, 256), vm(CUTS, WIDE, R0), vm(2, WIDE, HID), vm(2, HID, HID),
             vm(2, CLASSES, HID), vm(2, PADDED, HID),
             vm(CUTS, 144, 128), vm(CUTS, 144, 128), vm(2, CUTS, WIDE, 512), vm(2, 4, CUTS, WIDE, 128), vm(2, ROWS, R1),
             vf(R1, HID), vm(256, HID), vm(R2, HID), vf(R2, HID), vm(256, HID), vm(SEEDS, HID), vm(256, HID),
@@ -515,7 +542,7 @@
         compiler_params=pltpu.CompilerParams(
             collective_id=1, has_side_effects=True, vmem_limit_bytes=56 * 2**20
         ),
-    )(lists, xt, w_self, w_neigh, second_self, second_neigh, final_t, third_t, idx)
+    )(*operands)
 
 
 def finish_kernel(upper, lower, first_self, first_neigh, second_self, second_neigh, third_self, third_neigh):
@@ -547,15 +574,10 @@
     xt = jnp.swapaxes(features[0], 1, 2)
     lists = jnp.transpose(lists_one[0], (2, 0, 1))
 
-    def padded(v):
-        return jnp.pad(v, ((0, 0), (0, 256 - v.shape[1])), constant_values=-1)
-
-    idx = jnp.concatenate(
-        [padded(lists_two[0, 0].T), padded(lists_three[0, 0].T), padded(labels[0]), jnp.full((7, 256), -1, jnp.int32)]
-    )
     loss, upper, lower = step(
         lists, xt, initial_node_weight, initial_neighbour_weight, second_self, second_neigh,
-        final_node_weight.T, third_neigh.T, idx,
+        final_node_weight.T, third_neigh.T,
+        jnp.transpose(lists_two[0], (2, 0, 1)), jnp.transpose(lists_three[0], (2, 0, 1)), labels[0],
     )
     return (loss,) + tuple(finish(upper, lower))
 

time: 105 us -> 93.6 us (0.89)
  Pallas kernels: 100 us -> 91 us
  local copies, waits for them, and re-layouts: 1.45 us -> 0 us
  other arithmetic: 1.33 us -> 0 us
    pallas_call x1, Pallas kernels: 98 us -> 89 us  [step(): pl.pallas_call(kernel, out_shape=(jax.ShapeDtypeStruct((1, 1), F32), jax....]
    unnamed x2 -> x0, local copies, waits for them, and re-layouts: 1.37 us -> none
    concatenate x1 -> x0, other arithmetic: 1.33 us -> none  [per_device(): jnp.concatenate([padded(lists_two[0, 0].T), padded(lists_three[0, 0].T),...]
where the time goes in v3:
time: 93.6 us; the launch traced here: 93.4 us
  Pallas kernels  91 us (97%)
  between operations  2.41 us (3%)
    pallas_call x1, Pallas kernels, step(): pl.pallas_call(kernel, out_shape=(jax.ShapeDtypeStruct((1, 1), F32), jax....  89 us
    pallas_call x1, Pallas kernels, finish(): pl.pallas_call(finish_kernel, out_shape=tuple((jax.ShapeDtypeStruct(s, F3...  2.02 us

profile of v3, /device:TPU:1, one launch (start us, length us, event | category | flops | bytes accessed | tf_op | source)
XLA Modules:
  0.0 93.4 jit_solution(9279436650379216938)
XLA Ops:
  0.6 89.0 %shard_map.162 = (f32[1,1]{1,0:T(1,128)}, bf16[2,8,80,128]{3,2,1,0:T(8,128)(2,1)}, bf16[2,8,48,128]{3,2,1,0:T(8,128)(2,1)}) custom-call(s32[5,16,192]{2,1,0:T(8,128)} %bitcast.18, bf16[16,48,1024]{2,1,0:T(8,128)(2,1)} %bitcast.15, bf16[48,1024]{1,0:T(8,128)(2,1)} %w_self_hbm.1, bf16[48,1024]{1,0:T(8,128)(2,1)} %w_neigh_hbm.1, ...), custom_call_target="tpu_custom_call" | custom-call | tf_op jit(solution)/shard_map/pallas_call | solution.py:518
  89.7 2.0 %shard_map.163 = (f32[48,1024]{1,0:T(8,128)}, f32[48,1024]{1,0:T(8,128)}, f32[64,1024]{1,0:T(8,128)}, f32[64,1024]{1,0:T(8,128)}, f32[64,153]{1,0:T(8,128)}, /*index=5*/f32[64,153]{1,0:T(8,128)}) custom-call(bf16[2,8,80,128]{3,2,1,0:T(8,128)(2,1)} %get-tuple-element.17.upper, bf16[2,8,48,128]{3,2,1,0:T(8,128)(2,1)} %get-tuple-element.18.lower), custom_call_target="tpu_custom_call" | custom-call | tf_op jit(solution)/shard_map/pallas_call | solution.py:562

commit v4 on v3

--- a/solution.py
+++ b/solution.py
@@ -23,9 +23,9 @@
 PADDED = 256
 VMEM = pl.BlockSpec(memory_space=pltpu.VMEM)
 ANY = pl.BlockSpec(memory_space=pl.ANY)
-SLOTS = 192
-UPPER = (48, 32)
-LOWER = (16, 32)
+SLOTS = 80
+UPPER = (32, 32, 16)
+LOWER = (16, 16, 16)
 
 
 def dot(a, b):
@@ -61,9 +61,9 @@
     ra1, ra2, ra3, rg1, rg2, rg3,
     *rest,
 ):
-    bufs_a, bufs_b = rest[:13], rest[13:26]
-    rest_keep, rest_rz = rest[26:30], rest[30:32]
-    load, send, recv, a_send, a_recv = rest[32:]
+    bufs_a, bufs_b = rest[:17], rest[17:34]
+    rest_keep, rest_rz = rest[34:38], rest[38:42]
+    load, send, recv, a_send, a_recv = rest[42:]
     d, c = lax.axis_index("dp"), lax.axis_index("cuts")
     x, y, zh, zl, k = c // 4, d // 4, c % 4, (d // 2) % 2, d % 2
     me = c
@@ -76,12 +76,15 @@
 
     sibling = peer(dk=1)
     xs = [(x + s) % 4 for s in range(4)]
+    quads = [pl.ds(pl.multiple_of(v * 4, 4), 4) for v in xs]
+    behinds = [x * 4 + (zh + 4 - j) % 4 for j in range(4)]
     ys = [(y + s) % 4 for s in range(4)]
 
     barrier = pltpu.get_barrier_semaphore()
     peers = [peer(dx=s // 4, dzh=s % 4) for s in range(1, 16)]
     peers += [peer(dy=s // 2, dzl=s % 2) for s in range(1, 8)]
     peers += [peer(dzh=s, dzl=1) for s in range(1, 4)]
+    peers += [peer(dx=i, dy=j) for i in range(1, 4) for j in range(1, 4)]
     peers += [sibling]
     for p in peers:
         pl.semaphore_signal(barrier, 1, device_id=p, device_id_type=MESH)
@@ -112,40 +115,46 @@
 
     sends = []
 
+    def start(n, src, dst, to):
+        pltpu.make_async_remote_copy(
+            src_ref=src, dst_ref=dst, send_sem=send.at[n], recv_sem=recv.at[n], device_id=to, device_id_type=MESH
+        ).start()
+
+    def link_all(whole, copies):
+        n = len(sends)
+        sends.append(whole)
+        for src, dst, to in copies:
+            start(n, src, dst, to)
+        return n
+
     def link(src, dst, to):
-        n = len(sends)
-        cp = pltpu.make_async_remote_copy(
-            src_ref=src, dst_ref=dst, send_sem=send.at[n], recv_sem=recv.at[n], device_id=to, device_id_type=MESH
+        return link_all(src, [(src, dst, to)])
+
+    def pair_of(n, ref):
+        return pltpu.make_async_remote_copy(
+            src_ref=ref, dst_ref=ref, send_sem=send.at[n], recv_sem=recv.at[n], device_id=sibling, device_id_type=MESH
         )
-        cp.start()
-        sends.append(cp)
-        return n
 
     def arrived(n, dst):
-        pltpu.make_async_remote_copy(
-            src_ref=dst, dst_ref=dst, send_sem=send.at[n], recv_sem=recv.at[n], device_id=sibling, device_id_type=MESH
-        ).wait_recv()
+        pair_of(n, dst).wait_recv()
 
     for cp in ld_w:
         cp.wait()
-    for kk in range(2):
-        wa[kk, me] = w_in[kk, :, 0:512]
+    wa[k, me] = w_in[k, :, 0:512]
     wb[k, y, me] = w_in[k, :, pl.ds(pl.multiple_of(512 + y * 128, 128), 128)]
     ld_lists.wait()
     pl.semaphore_wait(barrier, len(peers))
 
     wbz = [link(wb.at[k, y, me], wb.at[k, y, me], peer(dzh=s)) for s in range(1, 4)]
+    def across(j):
+        src = wa.at[k, behinds[j]]
+        for s in range(1, 4):
+            start(wax[s - 1], src, src, peer(dx=s))
+
+    wax = [link_all(wa.at[k, quads[0]], []) for s in range(1, 4)]
     waz = [link(wa.at[k, me], wa.at[k, me], peer(dzh=s)) for s in range(1, 4)]
 
-    def spread_x(j):
-        src = x * 4 + (zh + 4 - j) % 4
-        return [link(wa.at[k, src], wa.at[k, src], peer(dx=s)) for s in range(1, 4)]
-
-    wx = {0: spread_x(0)}
-    wk = {}
-
-    def spread_core(key, src):
-        wk[key] = link(wa.at[k, src], wa.at[k, src], sibling)
+    across(0)
 
     def block(m):
         one, zero = jnp.ones((16, R1), BF), jnp.zeros((16, R1), BF)
@@ -166,48 +175,53 @@
         ref[m, 48:96] = mean[:, 0:128]
         ref[m, 96:144] = jnp.concatenate([own[:, 128:192], mean[:, 128:192]], axis=1)
 
-    def a_copy(s):
-        m = (me + s) % CUTS
+    def a_pair(s=None):
+        here = pl.ds(0, CUTS - 1) if s is None else s - 1
         return pltpu.make_async_remote_copy(
-            src_ref=blk_out.at[m], dst_ref=blk_in.at[me], send_sem=a_send.at[s - 1], recv_sem=a_recv.at[s - 1],
-            device_id={"dp": d, "cuts": m}, device_id_type=MESH,
+            src_ref=blk_out.at[here], dst_ref=blk_in.at[here], send_sem=a_send.at[0], recv_sem=a_recv.at[0],
+            device_id=sibling if s is None else {"dp": d, "cuts": (me + s) % CUTS}, device_id_type=MESH,
         )
 
     def one(s, _):
-        m = (me + s) % CUTS
         xt_copy(s).wait()
-        own, mean = block(m)
-        pack(blk_out, m, own, mean)
-        a_copy(s).start()
+        own, mean = block((me + s) % CUTS)
+        pack(blk_out, s - 1, own, mean)
+
+        @pl.when(s < CUTS)
+        def _():
+            a_pair(s).start()
+
+        @pl.when(s == 6)
+        def _():
+            for j in range(1, 4):
+                arrived(wbz[j - 1], wb.at[k, y, behinds[j]])
+            for s in range(1, 4):
+                wbx.append(link(wb.at[k, y, quads[0]], wb.at[k, y, quads[0]], peer(dx=s)))
+
+        @pl.when(s == 8)
+        def _():
+            for j in (1, 3):
+                arrived(waz[j - 1], wa.at[k, behinds[j]])
+                across(j)
+
+        @pl.when(s == 11)
+        def _():
+            for s in range(1, 4):
+                arrived(wbx[s - 1], wb.at[k, y, quads[-s]])
+            for s in range(1, 4):
+                wby.append(link(wb.at[k, y], wb.at[k, y], peer(dy=s)))
+            wbk.append(link(wb.at[k, y], wb.at[k, y], sibling))
+
+        @pl.when(s == 13)
+        def _():
+            arrived(waz[1], wa.at[k, behinds[2]])
+            across(2)
+            wak.append(link(wa.at[k, quads[0]], wa.at[k, quads[0]], sibling))
+
         return 0
 
-    def behind(j):
-        return x * 4 + (zh + 4 - j) % 4
-
-    def z_arrival(j):
-        arrived(waz[j - 1], wa.at[k, behind(j)])
-        wx[j] = spread_x(j)
-        spread_core((j, 0), behind(j))
-
-    def mine_x(dx):
-        return pl.ds(pl.multiple_of(((x + 4 + dx) % 4) * 4, 4), 4)
-
-    lax.fori_loop(1, 5, one, 0)
-    for j in range(1, 4):
-        arrived(wbz[j - 1], wb.at[k, y, behind(j)])
-    wbx = [link(wb.at[k, y, mine_x(0)], wb.at[k, y, mine_x(0)], peer(dx=s)) for s in range(1, 4)]
-    lax.fori_loop(5, 8, one, 0)
-    z_arrival(1)
-    z_arrival(3)
-    for s in range(1, 4):
-        arrived(wbx[s - 1], wb.at[k, y, mine_x(-s)])
-    wby = [link(wb.at[k, y], wb.at[k, y], peer(dy=s)) for s in range(1, 4)]
-    wbk = {0: link(wb.at[k, y], wb.at[k, y], sibling)}
-    z_arrival(2)
-    lax.fori_loop(8, 16, one, 0)
-    xt_copy(16).wait()
-    own, mean = block(me)
-    pack(blk_in, me, own, mean)
+    wbx, wby, wak, wbk = [], [], [], []
+    lax.fori_loop(1, CUTS + 1, one, 0)
 
     for cp in ld_top:
         cp.wait()
@@ -238,34 +252,29 @@
     act2[R2:256] = jnp.zeros((256 - R2, HID), BF)
     back2[R2:256] = jnp.zeros((256 - R2, HID), BF)
 
-    for j in (0, 1, 3, 2):
-        for s in range(1, 4):
-            src = ((x + 4 - s) % 4) * 4 + (zh + 4 - j) % 4
-            arrived(wx[j][s - 1], wa.at[k, src])
-            spread_core((j, s), src)
-    for s in range(1, CUTS):
-        frm = (me + CUTS - s) % CUTS
-        pltpu.make_async_remote_copy(
-            src_ref=blk_in.at[frm], dst_ref=blk_in.at[frm], send_sem=a_send.at[s - 1], recv_sem=a_recv.at[s - 1],
-            device_id=sibling, device_id_type=MESH,
-        ).wait_recv()
-    for i in range(CUTS):
-        tail = blk_in[i, 96:144]
-        at[0, i * 48:(i + 1) * 48, 0:128] = blk_in[i, 0:48]
-        at[1, i * 48:(i + 1) * 48, 0:128] = blk_in[i, 48:96]
-        at[0, i * 48:(i + 1) * 48, 128:192] = tail[:, 0:64]
-        at[1, i * 48:(i + 1) * 48, 128:192] = tail[:, 64:128]
+    for s in range(1, 4):
+        arrived(wax[s - 1], wa.at[k, quads[-s]])
+        wak.append(link(wa.at[k, quads[-s]], wa.at[k, quads[-s]], sibling))
+    a_pair().wait_recv()
+    for s in range(CUTS):
+        src, ref, i = (me + CUTS - s) % CUTS, blk_in if s else blk_out, s - 1 if s else CUTS - 1
+        here = pl.ds(pl.multiple_of(src * WIDE, WIDE), WIDE)
+        tail = ref[i, 96:144]
+        at[0, here, 0:128] = ref[i, 0:48]
+        at[1, here, 0:128] = ref[i, 48:96]
+        at[0, here, 128:192] = tail[:, 0:64]
+        at[1, here, 128:192] = tail[:, 64:128]
     sw_a1 = link(at.at[1 - k], ra1, sibling)
     at0, at1 = at[0].T, at[1].T
     for s in range(1, 4):
         frm = (y + 4 - s) % 4
         arrived(wby[s - 1], wb.at[k, frm])
-        wbk[s] = link(wb.at[k, frm], wb.at[k, frm], sibling)
+        wbk.append(link(wb.at[k, frm], wb.at[k, frm], sibling))
 
     for n in range(4):
         if n == 0:
-            for (j, s), number in wk.items():
-                arrived(number, wa.at[1 - k, ((x + 4 - s) % 4) * 4 + (zh + 4 - j) % 4])
+            for s in range(4):
+                arrived(wak[s], wa.at[1 - k, quads[-s]])
         if n == 2:
             for s in range(4):
                 arrived(wbk[s], wb.at[1 - k, (y + 4 - s) % 4])
@@ -353,11 +362,12 @@
         lax.fori_loop(0, dst.shape[0], body, 0)
 
     class Chunk:
-        def __init__(self, sizes, bufs, out):
-            self.rows, self.out = sizes, out
+        def __init__(self, sizes, bufs, out, back):
+            self.rows, self.out, self.back = sizes, out, back
             (
                 self.s1, self.s2, rel1, dir1, com1, rel2, dir2, com2, self.t1, self.t2, self.q1, self.q2, self.u,
-            ) = bufs[:13]
+                self.sz, self.rz1, self.tz, self.rt,
+            ) = bufs
             self.y = Ring(
                 lambda off, h: self.s1.at[ys[off], pl.ds(8 * h, 8)], add_leading, peer(dy=1), peer(dy=3), rel1, dir1, com1
             )
@@ -368,20 +378,46 @@
 
         def first_y_done(self):
             self.y.finish(lambda h: self.t1.at[pl.ds(8 * h, 8)])
-            self.n1 = [link(self.t1.at[mine_x(s)], self.q1.at[s - 1], peer(dx=s)) for s in range(1, 4)]
+            self.n1 = link_all(self.q1, [(self.t1.at[quads[s]], self.q1.at[s - 1], peer(dx=s)) for s in range(1, 4)])
 
         def first_x_done(self):
             self.x.finish(lambda h: self.t2.at[:, pl.ds(2 * h, 2)])
-            self.n2 = [link(self.t2.at[ys[s]], self.q2.at[s - 1], peer(dy=s)) for s in range(1, 4)]
+            self.n2 = link_all(self.q2, [(self.t2.at[ys[s]], self.q2.at[s - 1], peer(dy=s)) for s in range(1, 4)])
+
+        def fill_z(self, n, v):
+            for i in range(CUTS):
+                for h in range(2):
+                    self.sz[h, i % 4, i // 4, n] = v[i, :, lanes(h, 128)]
+
+        def z_first(self):
+            far = [(zl * 4 + zh + s) % 8 for s in range(1, 8)]
+            self.n6 = link_all(
+                self.rz1,
+                [(self.sz.at[p // 4, p % 4], self.rz1.at[s], device(x, y, p % 4, p // 4, k)) for s, p in enumerate(far)],
+            )
+
+        def z_sum(self):
+            arrived(self.n6, self.rz1)
+            for i in range(4):
+                v = self.sz[zl, zh, i].astype(F32)
+                for s in range(7):
+                    v = v + self.rz1[s, i].astype(F32)
+                self.tz[i] = v.astype(BF)
+            self.n7 = link_all(
+                self.rt,
+                [
+                    (self.tz.at[xs[q // 4], ys[q % 4]], self.rt.at[q - 1], peer(dx=q // 4, dy=q % 4))
+                    for q in range(1, 16)
+                ],
+            )
 
         def second_done(self, rz):
-            r1, r2 = self.rows
-            for lo, hi, numbers, t, q in (
+            r1, r2, _ = self.rows
+            for lo, hi, number, t, q in (
                 (0, r1, self.n1, lambda h: self.t1[x * 4 + h], self.q1),
                 (r1, r1 + r2, self.n2, lambda h: self.t2[y, h], self.q2),
             ):
-                for s in range(3):
-                    arrived(numbers[s], q.at[s])
+                arrived(number, q)
                 for h in range(4):
                     v = t(h).astype(F32)
                     for s in range(3):
@@ -390,43 +426,48 @@
                     self.u[0, h, lo:hi] = v[:, 0:128]
                     self.u[1, h, lo:hi] = v[:, 128:256]
             self.rz = rz
-            self.n3 = []
-            for s in range(1, 8):
-                p = (zl * 4 + zh + s) % 8
-                self.n3.append(link(self.u.at[p // 4, p % 4], rz.at[s - 1], device(x, y, p % 4, p // 4, k)))
+            far = [(zl * 4 + zh + s) % 8 for s in range(1, 8)]
+            self.n3 = link_all(
+                rz, [(self.u.at[p // 4, p % 4], rz.at[s], device(x, y, p % 4, p // 4, k)) for s, p in enumerate(far)]
+            )
 
         def third_done(self):
             v = self.u[zl, zh].astype(F32)
+            arrived(self.n3, self.rz)
             for s in range(7):
-                arrived(self.n3[s], self.rz.at[s])
                 v = v + self.rz[s].astype(F32)
             self.mine = y * 2 + zl
             piece = self.out.at[k, self.mine]
-            self.out[k, self.mine] = v.astype(BF)
-            self.n4 = []
+            rows = self.rows[0] + self.rows[1]
+            self.out[k, self.mine, 0:rows] = v.astype(BF)
+            arrived(self.n7, self.rt)
+            v = self.tz[x, y].astype(F32)
+            for s in range(15):
+                v = v + self.rt[s].astype(F32)
+            self.out[k, self.mine, rows:rows + 16] = v.astype(BF)
+            far = [(self.mine + s) % 8 for s in range(1, 8)]
+            self.n4 = link_all(
+                self.back, [(piece, self.back.at[s], device(x, p // 2, zh, p % 2, k)) for s, p in enumerate(far)]
+            )
+
+        def gathered(self):
+            arrived(self.n4, self.back)
             for s in range(1, 8):
-                p = (self.mine + s) % 8
-                self.n4.append(link(piece, piece, device(x, p // 2, zh, p % 2, k)))
-            self.n5 = [link(piece, piece, sibling)]
-
-        def gathered(self):
-            for s in range(1, 8):
-                piece = self.out.at[k, (self.mine + 8 - s) % 8]
-                arrived(self.n4[s - 1], piece)
-                self.n5.append(link(piece, piece, sibling))
+                self.out[k, (self.mine + 8 - s) % 8] = self.back[s - 1]
+            self.n5 = link(self.out.at[k], self.out.at[k], sibling)
 
         def done(self):
-            for s in range(8):
-                arrived(self.n5[s], self.out.at[1 - k, (self.mine + 8 - s) % 8])
-
-    upper, lower = Chunk(UPPER, bufs_a, out_a), Chunk(LOWER, bufs_b, out_b)
+            arrived(self.n5, self.out.at[1 - k])
+
+    upper, lower = Chunk(UPPER, bufs_a, out_a, rest_rz[2]), Chunk(LOWER, bufs_b, out_b, rest_rz[3])
     order = (2, 1, 3, 0)
 
     arrived(sw_g3, rg3)
     arrived(sw_a3, ra3)
     third = (dot(keep3[...].T, g3[...]) + dot(ra3[...].T, rg3[...])).astype(BF).reshape(CUTS, 4, 16, 256)
     for j in range(4):
-        upper.s2[j, :, 16:32] = third[:, j]
+        upper.fill_z(j, third[:, j])
+    upper.z_first()
     keep_t = keep2[...].T
     arrived(sw_a2, ra2)
     sib_t = ra2[...].T
@@ -434,8 +475,8 @@
     for off in order:
         n = ys[off]
         p = (dot(keep_t, g2[:, lanes(n)]) + dot(sib_t, rg2[:, lanes(n)])).astype(BF).reshape(CUTS, 64, 256)
-        upper.s1[n] = p[:, 0:48]
-        upper.s2[n, :, 0:16] = p[:, 48:64]
+        upper.s1[n] = p[:, 0:32]
+        upper.s2[n] = p[:, 32:64]
         if off == 2:
             upper.y.opposite()
         if off == 1:
@@ -462,7 +503,8 @@
         n = ys[off]
         p = (dot(at[k], g1[:, lanes(n)]) + dot(ra1[...], rg1[:, lanes(n)])).astype(BF).reshape(CUTS, 48, 256)
         lower.s1[n] = p[:, 0:16]
-        lower.s2[n] = p[:, 16:48]
+        lower.s2[n] = p[:, 16:32]
+        lower.fill_z(n, p[:, 32:48])
         if off == 2:
             lower.y.opposite()
         if off == 1:
@@ -470,32 +512,30 @@
             upper.x.pass_on()
         if off == 3:
             lower.y.to_down()
+    lower.z_first()
     lower.x.opposite()
     lower.x.to_up()
     lower.x.to_down()
     upper.first_y_done()
+    upper.first_x_done()
+    upper.z_sum()
     lower.y.pass_on()
-    upper.first_x_done()
     lower.x.pass_on()
     upper.second_done(rest_rz[0])
     lower.first_y_done()
     lower.first_x_done()
     upper.third_done()
     lower.second_done(rest_rz[1])
+    lower.z_sum()
     upper.gathered()
     lower.third_done()
     lower.gathered()
     upper.done()
     lower.done()
 
-    for cp in sends:
-        cp.wait_send()
-
-    def sent(s, _):
-        a_copy(s).wait_send()
-        return 0
-
-    lax.fori_loop(1, CUTS, sent, 0)
+    for n, ref in enumerate(sends):
+        pair_of(n, ref).wait_send()
+    a_pair().wait_send()
 
 
 def step(*operands):
@@ -505,7 +545,7 @@
     vi = lambda *shape: pltpu.VMEM(shape, jnp.int32)
 
     def chunk(sizes):
-        r1, r2 = sizes
+        r1, r2, r3 = sizes
         return [
             vm(4, CUTS, r1, 256), vm(4, CUTS, r2, 256),
             vm(2, 8, r1, 256), vm(2, 8, r1, 256), vm(2, 8, r1, 256),
@@ -513,6 +553,7 @@
             vm(CUTS, r1, 256), vm(4, 4, r2, 256),
             vm(3, 4, r1, 256), vm(3, 4, r2, 256),
             vm(2, 4, r1 + r2, 128),
+            vm(2, 4, 4, 4, r3, 128), vm(7, 4, 4, r3, 128), vm(4, 4, r3, 128), vm(15, r3, 128),
         ]
 
     return pl.pallas_call(
@@ -527,7 +568,7 @@
         scratch_shapes=[
             vi(FAN1, CUTS, R1), vi(FAN2, 1, R2), vi(FAN3, 1, SEEDS), vi(1, SEEDS), vi(16, 256), vm(CUTS, WIDE, R0), vm(2, WIDE, HID), vm(2, HID, HID),
             vm(2, CLASSES, HID), vm(2, PADDED, HID),
-            vm(CUTS, 144, 128), vm(CUTS, 144, 128), vm(2, CUTS, WIDE, 512), vm(2, 4, CUTS, WIDE, 128), vm(2, ROWS, R1),
+            vm(CUTS, 144, 128), vm(CUTS - 1, 144, 128), vm(2, CUTS, WIDE, 512), vm(2, 4, CUTS, WIDE, 128), vm(2, ROWS, R1),
             vf(R1, HID), vm(256, HID), vm(R2, HID), vf(R2, HID), vm(256, HID), vm(SEEDS, HID), vm(256, HID),
             vm(R1, HID), vm(R2, HID), vm(SEEDS, PADDED),
             vm(ROWS, R1), vm(R2, HID), vm(SEEDS, HID), vm(R1, HID), vm(R2, HID), vm(SEEDS, PADDED),
@@ -536,8 +577,8 @@
         + chunk(LOWER)
         + [
             vm(SEEDS, HID), vm(R2, HID), vm(SEEDS, HID), vm(R2, HID),
-            vm(7, sum(UPPER), 128), vm(7, sum(LOWER), 128),
-            dma((40,)), dma((SLOTS,)), dma((SLOTS,)), dma((15,)), dma((15,)),
+            vm(7, sum(UPPER[:2]), 128), vm(7, sum(LOWER[:2]), 128), vm(7, sum(UPPER), 128), vm(7, sum(LOWER), 128),
+            dma((33,)), dma((SLOTS,)), dma((SLOTS,)), dma((1,)), dma((1,)),
         ],
         compiler_params=pltpu.CompilerParams(
             collective_id=1, has_side_effects=True, vmem_limit_bytes=56 * 2**20

time: 93.6 us -> 86.6 us (0.925)
  Pallas kernels: 91 us -> 84.1 us
    pallas_call x1, Pallas kernels: 89 us -> 82.1 us  [step(): pl.pallas_call(kernel, out_shape=(jax.ShapeDtypeStruct((1, 1), F32), jax....]
where the time goes in v4:
time: 86.6 us; the launch traced here: 86.5 us
  Pallas kernels  84.1 us (97%)
  between operations  2.41 us (3%)
    pallas_call x1, Pallas kernels, step(): pl.pallas_call(kernel, out_shape=(jax.ShapeDtypeStruct((1, 1), F32), jax....  82.1 us
    pallas_call x1, Pallas kernels, finish(): pl.pallas_call(finish_kernel, out_shape=tuple((jax.ShapeDtypeStruct(s, F3...  2.02 us

profile of v4, /device:TPU:1, one launch (start us, length us, event | category | flops | bytes accessed | tf_op | source)
XLA Modules:
  0.0 86.5 jit_solution(13110043021005868532)
XLA Ops:
  0.6 82.1 %shard_map.162 = (f32[1,1]{1,0:T(1,128)}, bf16[2,8,80,128]{3,2,1,0:T(8,128)(2,1)}, bf16[2,8,48,128]{3,2,1,0:T(8,128)(2,1)}) custom-call(s32[5,16,192]{2,1,0:T(8,128)} %bitcast.18, bf16[16,48,1024]{2,1,0:T(8,128)(2,1)} %bitcast.15, bf16[48,1024]{1,0:T(8,128)(2,1)} %w_self_hbm.1, bf16[48,1024]{1,0:T(8,128)(2,1)} %w_neigh_hbm.1, ...), custom_call_target="tpu_custom_call" | custom-call | tf_op jit(solution)/shard_map/pallas_call | solution.py:559
  82.7 2.0 %shard_map.163 = (f32[48,1024]{1,0:T(8,128)}, f32[48,1024]{1,0:T(8,128)}, f32[64,1024]{1,0:T(8,128)}, f32[64,1024]{1,0:T(8,128)}, f32[64,153]{1,0:T(8,128)}, /*index=5*/f32[64,153]{1,0:T(8,128)}) custom-call(bf16[2,8,80,128]{3,2,1,0:T(8,128)(2,1)} %get-tuple-element.17.upper, bf16[2,8,48,128]{3,2,1,0:T(8,128)(2,1)} %get-tuple-element.18.lower), custom_call_target="tpu_custom_call" | custom-call | tf_op jit(solution)/shard_map/pallas_call | solution.py:603

commit v5 on v4

--- a/solution.py
+++ b/solution.py
@@ -23,7 +23,7 @@
 PADDED = 256
 VMEM = pl.BlockSpec(memory_space=pltpu.VMEM)
 ANY = pl.BlockSpec(memory_space=pl.ANY)
-SLOTS = 80
+SLOTS = 67
 UPPER = (32, 32, 16)
 LOWER = (16, 16, 16)
 
@@ -146,6 +146,7 @@
     pl.semaphore_wait(barrier, len(peers))
 
     wbz = [link(wb.at[k, y, me], wb.at[k, y, me], peer(dzh=s)) for s in range(1, 4)]
+
     def across(j):
         src = wa.at[k, behinds[j]]
         for s in range(1, 4):
@@ -471,6 +472,8 @@
     keep_t = keep2[...].T
     arrived(sw_a2, ra2)
     sib_t = ra2[...].T
+    for n in range(4):
+        back2[0:R2, lanes(n)] = (dot_nt(g2[...], second[1, lanes(n), :]) * (1.0 / FAN2)).astype(BF)
     arrived(sw_g2, rg2)
     for off in order:
         n = ys[off]
@@ -488,15 +491,12 @@
     upper.x.to_down()
 
     for n in range(4):
-        back2[0:R2, lanes(n)] = (dot_nt(g2[...], second[1, lanes(n), :]) * (1.0 / FAN2)).astype(BF)
-    for n in range(4):
         own = dot_nt(g2[...], second[0, lanes(n), :])
         grad = dot(counts2t[:R1], back2[:, lanes(n)]) + jnp.concatenate(
             [own, jnp.zeros((R1 - R2, 256), F32)], axis=0
         )
         g1[:, lanes(n)] = (grad * slope(pre1[:, lanes(n)])).astype(BF)
     sw_g1 = link(g1, rg1, sibling)
-    upper.y.pass_on()
     arrived(sw_a1, ra1)
     arrived(sw_g1, rg1)
     for off in order:
@@ -509,9 +509,10 @@
             lower.y.opposite()
         if off == 1:
             lower.y.to_up()
-            upper.x.pass_on()
+            upper.y.pass_on()
         if off == 3:
             lower.y.to_down()
+            upper.x.pass_on()
     lower.z_first()
     lower.x.opposite()
     lower.x.to_up()
@@ -524,11 +525,11 @@
     upper.second_done(rest_rz[0])
     lower.first_y_done()
     lower.first_x_done()
-    upper.third_done()
     lower.second_done(rest_rz[1])
     lower.z_sum()
+    upper.third_done()
+    lower.third_done()
     upper.gathered()
-    lower.third_done()
     lower.gathered()
     upper.done()
     lower.done()

time: 86.6 us -> 85.3 us (0.985)
  Pallas kernels: 84.1 us -> 82.7 us
    pallas_call x1, Pallas kernels: 82.1 us -> 80.7 us  [step(): pl.pallas_call(kernel, out_shape=(jax.ShapeDtypeStruct((1, 1), F32), jax....]
where the time goes in v5:
time: 85.3 us; the launch traced here: 85.2 us
  Pallas kernels  82.7 us (97%)
  between operations  2.41 us (3%)
    pallas_call x1, Pallas kernels, step(): pl.pallas_call(kernel, out_shape=(jax.ShapeDtypeStruct((1, 1), F32), jax....  80.7 us
    pallas_call x1, Pallas kernels, finish(): pl.pallas_call(finish_kernel, out_shape=tuple((jax.ShapeDtypeStruct(s, F3...  2.02 us

profile of v5, /device:TPU:1, one launch (start us, length us, event | category | flops | bytes accessed | tf_op | source)
XLA Modules:
  0.0 85.2 jit_solution(2273639974320553789)
XLA Ops:
  0.6 80.7 %shard_map.162 = (f32[1,1]{1,0:T(1,128)}, bf16[2,8,80,128]{3,2,1,0:T(8,128)(2,1)}, bf16[2,8,48,128]{3,2,1,0:T(8,128)(2,1)}) custom-call(s32[5,16,192]{2,1,0:T(8,128)} %bitcast.18, bf16[16,48,1024]{2,1,0:T(8,128)(2,1)} %bitcast.15, bf16[48,1024]{1,0:T(8,128)(2,1)} %w_self_hbm.1, bf16[48,1024]{1,0:T(8,128)(2,1)} %w_neigh_hbm.1, ...), custom_call_target="tpu_custom_call" | custom-call | tf_op jit(solution)/shard_map/pallas_call | solution.py:560
  81.4 2.0 %shard_map.163 = (f32[48,1024]{1,0:T(8,128)}, f32[48,1024]{1,0:T(8,128)}, f32[64,1024]{1,0:T(8,128)}, f32[64,1024]{1,0:T(8,128)}, f32[64,153]{1,0:T(8,128)}, /*index=5*/f32[64,153]{1,0:T(8,128)}) custom-call(bf16[2,8,80,128]{3,2,1,0:T(8,128)(2,1)} %get-tuple-element.17.upper, bf16[2,8,48,128]{3,2,1,0:T(8,128)(2,1)} %get-tuple-element.18.lower), custom_call_target="tpu_custom_call" | custom-call | tf_op jit(solution)/shard_map/pallas_call | solution.py:604

commit v6 on v5

--- a/solution.py
+++ b/solution.py
@@ -101,8 +101,17 @@
     ld_idx = [fetch(lists2_hbm, lists2), fetch(lists3_hbm, lists3), fetch(labels_hbm, labels)]
     ld_w = [fetch(w_self_hbm, w_in.at[0]), fetch(w_neigh_hbm, w_in.at[1])]
 
+    def ahead(s):
+        q = s - 1
+        far = 1 - q // 12
+        return far * (q // 3) + (1 - far) * (q - 11), far * (1 + q % 3)
+
+    def cut_ahead(s):
+        dx, dz = ahead(s)
+        return (x + dx) % 4 * 4 + (zh + dz) % 4
+
     def xt_copy(s):
-        m = (me + s) % CUTS
+        m = cut_ahead(s)
         return pltpu.make_async_copy(xt_hbm.at[m], xt.at[m], load.at[16 + s])
 
     def xt_start(s, _):
@@ -143,20 +152,6 @@
     wa[k, me] = w_in[k, :, 0:512]
     wb[k, y, me] = w_in[k, :, pl.ds(pl.multiple_of(512 + y * 128, 128), 128)]
     ld_lists.wait()
-    pl.semaphore_wait(barrier, len(peers))
-
-    wbz = [link(wb.at[k, y, me], wb.at[k, y, me], peer(dzh=s)) for s in range(1, 4)]
-
-    def across(j):
-        src = wa.at[k, behinds[j]]
-        for s in range(1, 4):
-            start(wax[s - 1], src, src, peer(dx=s))
-
-    wax = [link_all(wa.at[k, quads[0]], []) for s in range(1, 4)]
-    waz = [link(wa.at[k, me], wa.at[k, me], peer(dzh=s)) for s in range(1, 4)]
-
-    across(0)
-
     def block(m):
         one, zero = jnp.ones((16, R1), BF), jnp.zeros((16, R1), BF)
         wanted = [jnp.broadcast_to(lists[f, pl.ds(m, 1), :], (16, R1)).astype(jnp.int16) for f in range(FAN1)]
@@ -176,17 +171,38 @@
         ref[m, 48:96] = mean[:, 0:128]
         ref[m, 96:144] = jnp.concatenate([own[:, 128:192], mean[:, 128:192]], axis=1)
 
+    def prepare(s, _):
+        xt_copy(s).wait()
+        own, mean = block(cut_ahead(s))
+        pack(blk_out, s - 1, own, mean)
+        return 0
+
+    lax.fori_loop(1, 4, prepare, 0)
+    pl.semaphore_wait(barrier, len(peers))
+
+    wbz = [link(wb.at[k, y, me], wb.at[k, y, me], peer(dzh=s)) for s in range(1, 4)]
+
+    def across(j):
+        src = wa.at[k, behinds[j]]
+        for s in range(1, 4):
+            start(wax[s - 1], src, src, peer(dx=s))
+
+    wax = [link_all(wa.at[k, quads[0]], []) for s in range(1, 4)]
+    waz = [link(wa.at[k, me], wa.at[k, me], peer(dzh=s)) for s in range(1, 4)]
+
+    across(0)
+
     def a_pair(s=None):
         here = pl.ds(0, CUTS - 1) if s is None else s - 1
         return pltpu.make_async_remote_copy(
             src_ref=blk_out.at[here], dst_ref=blk_in.at[here], send_sem=a_send.at[0], recv_sem=a_recv.at[0],
-            device_id=sibling if s is None else {"dp": d, "cuts": (me + s) % CUTS}, device_id_type=MESH,
+            device_id=sibling if s is None else {"dp": d, "cuts": cut_ahead(s)}, device_id_type=MESH,
         )
 
     def one(s, _):
-        xt_copy(s).wait()
-        own, mean = block((me + s) % CUTS)
-        pack(blk_out, s - 1, own, mean)
+        @pl.when(s >= 4)
+        def _():
+            prepare(s, 0)
 
         @pl.when(s < CUTS)
         def _():
@@ -257,8 +273,9 @@
         arrived(wax[s - 1], wa.at[k, quads[-s]])
         wak.append(link(wa.at[k, quads[-s]], wa.at[k, quads[-s]], sibling))
     a_pair().wait_recv()
-    for s in range(CUTS):
-        src, ref, i = (me + CUTS - s) % CUTS, blk_in if s else blk_out, s - 1 if s else CUTS - 1
+    for s in range(1, CUTS + 1):
+        dx, dz = ahead(s)
+        src, ref, i = (x + 8 - dx) % 4 * 4 + (zh + 4 - dz) % 4, blk_in if s < CUTS else blk_out, s - 1
         here = pl.ds(pl.multiple_of(src * WIDE, WIDE), WIDE)
         tail = ref[i, 96:144]
         at[0, here, 0:128] = ref[i, 0:48]

time: 85.3 us -> 85.5 us (level)
  no operation moved by 1% of the time
where the time goes in v6:
time: 85.5 us; the launch traced here: 85.4 us
  Pallas kernels  83 us (97%)
  between operations  2.41 us (3%)
    pallas_call x1, Pallas kernels, step(): pl.pallas_call(kernel, out_shape=(jax.ShapeDtypeStruct((1, 1), F32), jax....  81 us
    pallas_call x1, Pallas kernels, finish(): pl.pallas_call(finish_kernel, out_shape=tuple((jax.ShapeDtypeStruct(s, F3...  2.02 us

profile of v6, /device:TPU:1, one launch (start us, length us, event | category | flops | bytes accessed | tf_op | source)
XLA Modules:
  0.0 85.4 jit_solution(11067577527573137565)
XLA Ops:
  0.6 81.0 %shard_map.162 = (f32[1,1]{1,0:T(1,128)}, bf16[2,8,80,128]{3,2,1,0:T(8,128)(2,1)}, bf16[2,8,48,128]{3,2,1,0:T(8,128)(2,1)}) custom-call(s32[5,16,192]{2,1,0:T(8,128)} %bitcast.18, bf16[16,48,1024]{2,1,0:T(8,128)(2,1)} %bitcast.15, bf16[48,1024]{1,0:T(8,128)(2,1)} %w_self_hbm.1, bf16[48,1024]{1,0:T(8,128)(2,1)} %w_neigh_hbm.1, ...), custom_call_target="tpu_custom_call" | custom-call | tf_op jit(solution)/shard_map/pallas_call | solution.py:577
  81.6 2.0 %shard_map.163 = (f32[48,1024]{1,0:T(8,128)}, f32[48,1024]{1,0:T(8,128)}, f32[64,1024]{1,0:T(8,128)}, f32[64,1024]{1,0:T(8,128)}, f32[64,153]{1,0:T(8,128)}, /*index=5*/f32[64,153]{1,0:T(8,128)}) custom-call(bf16[2,8,80,128]{3,2,1,0:T(8,128)(2,1)} %get-tuple-element.17.upper, bf16[2,8,48,128]{3,2,1,0:T(8,128)(2,1)} %get-tuple-element.18.lower), custom_call_target="tpu_custom_call" | custom-call | tf_op jit(solution)/shard_map/pallas_call | solution.py:621
